TPU v7x, 256 devices: a whole 4x4x8 slice. The times are simulated.
256 devices in a mesh: grp: 8 (over x, core), slab: 32 (over y, z).
Axes of the slice: x: 4, y: 4, z: 8, core: 2. Of those that a mesh axis runs over, the one named last changes fastest.
Arguments:
- pre: bfloat16 [128, 128, 64, 128], P('slab', 'grp'), may hold values from -6 to 6
- cotan: bfloat16 [128, 128, 64, 128], P('slab', 'grp'), may hold values from -6 to 6
- pointwise: bfloat16 [64, 64], replicated, may hold values from -0.75 to 0.75
- spectral: bfloat16 [32, 32, 32, 64, 128], P('slab', 'grp'), may hold values from -0.5 to 0.5
- w_in: float32 [6, 512], replicated, may hold values from -2.5 to 2.5
- b_in: float32 [512], replicated, may hold values from -3 to 3
- w_mid: float32 [512, 256], replicated, may hold values from -0.25 to 0.25
- b_mid: float32 [256], replicated, may hold values from -3 to 3
- w_out: float32 [256, 64], replicated, may hold values from -0.375 to 0.375
- b_out: float32 [64], replicated, may hold values from -3 to 3
- kernel_inputs: float32 [6, 262144], P(None, ('grp', 'slab')), may hold values from -1 to 1
- voxel_index: int32 [262144], P(('grp', 'slab')), may hold values from 0 to 8191
- routes: int32 [262144, 1], P(('grp', 'slab')), may hold values from 0 to 255; in each aligned block of 1024 rows (0 to 1023, 1024 to 2047, ...) at most 8 rows name the same one
- targets: int32 [262144], P(('grp', 'slab')), may hold values from 0 to 1023
- counts: int32 [2048], P(('grp', 'slab')), may hold values from 96 to 128
Outputs:
- d_features: float32 [64, 262144], P(None, ('grp', 'slab'))
Inputs may be any that keep to these rules, and one draw needn't show every extreme that they name: `voxel_index`: a flat index (first, second, third dimension order) into the block of 128/32 by 128/8 by 128 voxels held by the slot's device. `routes`: devices are numbered grp index times 32 plus slab index; among the slots of one device no more than 8 name one device, padded slots included. `counts`: slots of a block at or beyond its count are padding.
All inputs are finite; a program needn't handle non-finite values.
Results may differ from a plain program's by a relative error of at most 0.00035.
Values sent between devices are 32-bit elements; how exact they have to be, the bound alone decides.
No kernel may reach another device: no remote copies, remote signals or barrier semaphores. Data moves between devices by JAX's collectives and lax.ppermute only.
A program may use at most 64 MiB of HBM per device.

v0:
```python
import functools
import math

import jax
import jax.numpy as jnp
import numpy as np
from jax import lax
from jax.experimental import pallas as pl
from jax.experimental.pallas import tpu as pltpu
from jax.sharding import PartitionSpec as P

F32 = jnp.float32
BF16 = jnp.bfloat16
NG = 128
MODES = 32
CH = 64
NN = (((1,), (0,)), ((), ()))
NT = (((1,), (1,)), ((), ()))
TN = (((0,), (0,)), ((), ()))


def dot(a, b, dims=NN, precision=None):
    return lax.dot_general(a, b, dims, precision=precision, preferred_element_type=F32)


def tables():
    position = np.arange(NG)
    frequency = np.arange(MODES) - MODES // 2
    angle = (np.outer(frequency, position) % NG) * (2.0 * math.pi / NG)
    parts = []
    for table in (np.cos(angle), np.sin(angle)):
        high = table.astype(np.float32).astype(BF16)
        low = (table - high.astype(np.float64)).astype(np.float32).astype(BF16)
        parts.append((high, low))
    (ch, cl), (sh, sl) = parts
    zero = np.zeros_like(ch)
    forward = np.block([[ch, ch], [sh, sh], [cl, zero], [sl, zero]])
    inverse = np.concatenate([ch.T, ch.T, cl.T, sh.T, sh.T, sl.T], axis=1)
    return forward, inverse


def split(x):
    high = x.astype(BF16)
    return high, (x - high.astype(F32)).astype(BF16)


def lanes_of(shape):
    return lax.broadcasted_iota(jnp.int32, shape, len(shape) - 1)


def swap(x):
    return pltpu.roll(x, 64, 1)


def turn(x):
    return jnp.where(lanes_of(x.shape) < 64, swap(x), -swap(x))


def gelu(x):
    return 0.5 * x * (1.0 + lax.erf(x * (1.0 / math.sqrt(2.0))))


def forward_parts(product, first, width):
    at = slice(first, first + width)
    cos_part = product[0:32, at] + product[64:96, at]
    sin_part = product[32:64, at] + product[96:128, at]
    return cos_part, sin_part


def modes_z_kernel(pre_ref, cotan_ref, table_ref, out_ref, grad_ref):
    step = pl.program_id(0)
    pre = pre_ref[...].astype(F32).reshape(512, 128)
    cotan = cotan_ref[...].astype(F32).reshape(512, 128)
    cdf = 0.5 * (1.0 + lax.erf(pre * (1.0 / math.sqrt(2.0))))
    grad = cotan * (cdf + pre * jnp.exp(-0.5 * pre * pre) * (1.0 / math.sqrt(2.0 * math.pi)))
    high, low = split(grad)
    both = jnp.concatenate([high, low], axis=1)
    grad_ref[...] = both
    product = dot(table_ref[...], both, NT)
    for pair in range(4):
        real, minus = forward_parts(product, pair * 128, 128)
        imag = -minus
        left = lanes_of(real.shape) < 64
        row = step * 8 + 2 * pair
        out_ref[pl.ds(row, 32, stride=64), :] = jnp.where(left, real, swap(imag))
        out_ref[pl.ds(row + 1, 32, stride=64), :] = jnp.where(left, swap(real), imag)


def modes_x_kernel(in_ref, table_ref, out_ref):
    for y in range(0, 16, 2):
        data = jnp.concatenate([in_ref[pl.ds(y + h, 128, stride=16), :] for h in range(2)], axis=1)
        high, low = split(data)
        product = dot(table_ref[...], jnp.concatenate([high, low], axis=0))
        for h in range(2):
            cos_part, sin_part = forward_parts(product, h * 128, 128)
            out_ref[pl.ds(y + h, 32, stride=16), :] = cos_part + turn(sin_part)


def inverse_stack(mixed):
    mixed_high, mixed_low = split(mixed)
    high, low = split(-turn(mixed))
    return jnp.concatenate([mixed_high, mixed_low, mixed_high, high, low, high], axis=0)


def mix_kernel(in_ref, spectral_ref, forward_ref, inverse_ref, out_ref):
    for kx in range(4):
        data = jnp.concatenate(
            [in_ref[g * 64 + kx * 16 : g * 64 + kx * 16 + 16, :] for g in range(8)], axis=0
        )
        high, low = split(data)
        product = dot(forward_ref[...], jnp.concatenate([high, low], axis=0))
        cos_part, sin_part = forward_parts(product, 0, 128)
        hat = cos_part + turn(sin_part)
        other = turn(hat)
        halves = []
        for part in range(2):
            at = slice(part * 16, part * 16 + 16)
            high, low = split(jnp.concatenate([hat[at], other[at]], axis=0))
            first = (kx * 32 + part * 16) * 64
            cross = dot(
                jnp.concatenate([high, low], axis=0), spectral_ref[first : first + 1024, :], NT
            )
            cross = cross[:32] + cross[32:]
            row = lax.broadcasted_iota(jnp.int32, (16, 128), 0)
            real = jnp.zeros((16, 128), F32)
            imag = jnp.zeros((16, 128), F32)
            for pair in range(8):
                own = (row >> 1) == pair
                at = slice(pair * 128, pair * 128 + 128)
                real = jnp.where(own, cross[:16, at], real)
                imag = jnp.where(own, cross[16:, at], imag)
            even = (row & 1) == 0
            left = lanes_of((16, 128)) < 64
            halves.append(
                jnp.where(
                    left,
                    jnp.where(even, real, swap(real)),
                    jnp.where(even, swap(imag), imag),
                )
            )
        mixed = jnp.concatenate(halves, axis=0) * (1.0 / float(NG) ** 3)
        field = dot(inverse_ref[...], inverse_stack(mixed))
        for g in range(8):
            out_ref[g * 64 + kx * 16 : g * 64 + kx * 16 + 16, :] = field[g * 16 : g * 16 + 16]


def field_x_kernel(in_ref, table_ref, out_ref):
    for y in range(0, 16, 2):
        stack = jnp.concatenate(
            [inverse_stack(in_ref[pl.ds(y + h, 32, stride=16), :]) for h in range(2)], axis=1
        )
        field = dot(table_ref[...], stack)
        for h in range(2):
            out_ref[pl.ds(y + h, 128, stride=16), :] = field[:, h * 128 : h * 128 + 128]


def rank_kernel(dest_ref, target_ref, code_ref, send_ref):
    dest = dest_ref[...]
    hit = lax.broadcasted_iota(jnp.int32, (256, 1024), 0) == dest
    one_hot = jnp.where(hit, 1.0, 0.0).astype(BF16)
    earlier = lax.broadcasted_iota(jnp.int32, (1024, 1024), 0) < lanes_of((1024, 1024))
    count = dot(one_hot, jnp.where(earlier, 1.0, 0.0).astype(BF16))
    rank = jnp.sum(jnp.where(hit, count, 0.0), axis=0, keepdims=True).astype(jnp.int32)
    code_ref[...] = (dest * 5 + (rank >> 1)) * 2 + (rank & 1)
    number = target_ref[...] + 1
    own = lax.broadcasted_iota(jnp.int32, (128, 1024), 0) == rank
    coarse = jnp.where(own, ((number >> 5) << 5).astype(F32), 0.0).astype(BF16)
    fine = jnp.where(own, (number & 31).astype(F32), 0.0).astype(BF16)
    send_ref[...] = dot(one_hot, coarse, NT) + dot(one_hot, fine, NT) - 1.0


def kernel_net_kernel(
    in_ref, w_in_ref, w_mid_ref, b_mid_ref, w_out_ref, b_out_ref, counts_ref, out_ref
):
    high = lax.Precision.HIGH
    for block in range(4):
        at = slice(block * 256, block * 256 + 256)
        hidden = gelu(dot(in_ref[:, at], w_in_ref[...], TN, high))
        hidden = gelu(dot(hidden, w_mid_ref[...], NN, high) + b_mid_ref[...])
        value = dot(hidden, w_out_ref[...], NT, high) + b_out_ref[...]
        for part in range(2):
            row = lax.broadcasted_iota(jnp.int32, (128, 128), 0)
            out_ref[block * 256 + part * 128 : block * 256 + part * 128 + 128, :] = jnp.where(
                row < counts_ref[block * 2 + part], value[part * 128 : part * 128 + 128], 0.0
            )


def local_kernel(grad_ref, weight_ref, voxel_ref, out_ref, table_ref):
    def fill(step, carry):
        for part in range(4):
            cell = step * 4 + part
            grad = grad_ref[pl.ds(pl.multiple_of(cell * 64, 64), 64), :]
            stack = jnp.concatenate([grad[:, :128], grad[:, 128:]], axis=0)
            rows = dot(weight_ref[...], stack)
            table_ref[pl.ds(pl.multiple_of(cell * 128, 128), 128), :] = rows.T
        return carry

    lax.fori_loop(0, 16, fill, 0)

    def take(step, carry):
        for part in range(16):
            slot = step * 16 + part
            out_ref[pl.ds(slot, 1), :] = table_ref[pl.ds(voxel_ref[slot], 1), :]
        return carry

    lax.fori_loop(0, 64, take, 0)


def slots_kernel(
    in_ref, table_ref, kernel_ref, local_ref, targets_ref, code_ref, voxel_ref, out_ref, field_ref
):
    out_ref[...] = jnp.zeros_like(out_ref)
    out_ref[pl.ds(4, 256, stride=5), :] = targets_ref[...]

    def fill(step, carry):
        for part in range(4):
            stacks = []
            first = step * 8 + part * 2
            for h in range(2):
                data = in_ref[pl.ds(first + h, 32, stride=64), :]
                other = swap(data)
                left = lanes_of(data.shape) < 64
                real_high, real_low = split(jnp.where(left, data, other))
                imag_high, imag_low = split(-jnp.where(left, other, data))
                stacks.append(
                    jnp.concatenate(
                        [real_high, real_low, real_high, imag_high, imag_low, imag_high], axis=0
                    )
                )
            field = dot(table_ref[...], jnp.concatenate(stacks, axis=1))
            for h in range(2):
                at = pl.multiple_of((first + h) * 128, 128)
                field_ref[pl.ds(at, 128), :] = field[:, h * 128 : h * 128 + 128]
        return carry

    lax.fori_loop(0, 8, fill, 0)
    side = lanes_of((1, 128)) >> 6

    def place(step, carry):
        for part in range(16):
            slot = step * 16 + part
            code = code_ref[slot]
            value = (
                field_ref[pl.ds(voxel_ref[slot], 1), :] + local_ref[pl.ds(slot, 1), :]
            ) * kernel_ref[pl.ds(slot, 1), :]
            pltpu.store(out_ref.at[pl.ds(code >> 1, 1), :], value, mask=side == (code & 1))
        return carry

    lax.fori_loop(0, 64, place, 0)


def gather_kernel(in_ref, out_ref):
    targets = in_ref[pl.ds(4, 256, stride=5), :]
    point = lanes_of((256, 1024)).astype(F32)
    total = jnp.zeros((128, 1024), F32)
    for pair in range(4):
        data = in_ref[pl.ds(pair, 256, stride=5), :].T
        high, low = split(data)
        for h in range(2):
            at = slice(h * 64, h * 64 + 64)
            column = targets[:, pair * 2 + h : pair * 2 + h + 1]
            one_hot = jnp.where(column == point, 1.0, 0.0).astype(BF16)
            total = total + dot(jnp.concatenate([high[at], low[at]], axis=0), one_hot)
    out_ref[...] = total[:64] + total[64:]


VMEM = pl.BlockSpec(memory_space=pltpu.VMEM)
SMEM = pl.BlockSpec(memory_space=pltpu.SMEM)
LIMIT = 48 * 1024 * 1024


def call(body, out_shape, in_specs, scratch=(), **more):
    return pl.pallas_call(
        body,
        out_shape=out_shape,
        in_specs=in_specs,
        scratch_shapes=list(scratch),
        compiler_params=pltpu.CompilerParams(vmem_limit_bytes=LIMIT),
        **more,
    )


def exchange(rows, axis, members):
    count = rows.shape[0] // members
    moved = lax.all_to_all(
        rows.reshape(members, count, 128), axis, split_axis=0, concat_axis=0, tiled=True
    )
    return moved.reshape(rows.shape)


def local(
    pre,
    cotan,
    pointwise,
    spectral,
    w_in,
    b_in,
    w_mid,
    b_mid,
    w_out,
    b_out,
    kernel_inputs,
    voxel_index,
    routes,
    targets,
    counts,
):
    forward, inverse = tables()
    forward, inverse = jnp.asarray(forward), jnp.asarray(inverse)
    shape = jax.ShapeDtypeStruct

    block = pl.BlockSpec((8, 64, 128), lambda i: (i, 0, 0))
    whole = pl.BlockSpec((128, 256), lambda i: (0, 0))
    columns, grad = call(
        modes_z_kernel,
        (shape((2048, 128), F32), shape((4096, 256), BF16)),
        [block, block, whole],
        grid=(8,),
        out_specs=(
            pl.BlockSpec((2048, 128), lambda i: (0, 0)),
            pl.BlockSpec((512, 256), lambda i: (i, 0)),
        ),
    )(pre.reshape(64, 64, 128), cotan.reshape(64, 64, 128), forward)

    routes, targets, kernel_inputs, grad = lax.optimization_barrier(
        (routes, targets, kernel_inputs, grad)
    )
    code, send_targets = call(
        rank_kernel,
        (shape((1, 1024), jnp.int32), shape((256, 128), F32)),
        [VMEM, VMEM],
    )(routes.reshape(1, 1024), targets.reshape(1, 1024))
    code = code.reshape(1024)
    net_in = jnp.concatenate([kernel_inputs, jnp.ones((1, 1024), F32), jnp.zeros((1, 1024), F32)])
    first_layer = jnp.concatenate([w_in, b_in[None], jnp.zeros((1, 512), F32)])
    kernel = call(
        kernel_net_kernel, shape((1024, 128), F32), [VMEM] * 6 + [SMEM]
    )(
        net_in,
        first_layer,
        w_mid,
        b_mid[None],
        jnp.concatenate([w_out.T, w_out.T]),
        jnp.concatenate([b_out, b_out])[None],
        counts,
    )
    weight = jnp.concatenate([pointwise, pointwise], axis=0)
    weight = jnp.concatenate([weight, weight], axis=1)
    own = call(
        local_kernel,
        shape((1024, 128), F32),
        [VMEM, VMEM, SMEM],
        [pltpu.VMEM((8192, 128), F32)],
    )(grad, weight, voxel_index)

    columns = exchange(columns, "slab", 32)
    rows = call(modes_x_kernel, shape((512, 128), F32), [VMEM, VMEM])(columns, forward)
    rows = exchange(rows, "grp", 8)
    rows = call(mix_kernel, shape((512, 128), F32), [VMEM] * 4)(
        rows, spectral.reshape(8192, 128), forward, inverse
    )
    rows = exchange(rows, "grp", 8)
    columns = call(field_x_kernel, shape((2048, 128), F32), [VMEM, VMEM])(rows, inverse)
    columns = exchange(columns, "slab", 32)
    slots = call(
        slots_kernel,
        shape((1280, 128), F32),
        [VMEM] * 5 + [SMEM] * 2,
        [pltpu.VMEM((8192, 128), F32)],
    )(columns, inverse, kernel, own, send_targets, code, voxel_index)
    slots = exchange(slots, ("grp", "slab"), 256)
    return call(gather_kernel, shape((64, 1024), F32), [VMEM])(slots)


def solution(mesh):
    placed = (
        P("slab", "grp", None, None),
        P("slab", "grp", None, None),
        P(),
        P("slab", "grp", None, None, None),
        P(),
        P(),
        P(),
        P(),
        P(),
        P(),
        P(None, ("grp", "slab")),
        P(("grp", "slab")),
        P(("grp", "slab"), None),
        P(("grp", "slab")),
        P(("grp", "slab")),
    )
    return jax.shard_map(
        local, mesh=mesh, in_specs=placed, out_specs=P(None, ("grp", "slab")), check_vma=False
    )
```

profile of v0, /device:TPU:1, one launch (start us, length us, event | category | flops | bytes accessed | tf_op | source)
XLA Modules:
  0.0 154.8 jit_solution(6261713278280992737)
XLA Ops:
  0.0 1.2 copy-done.3
  1.2 1.2 copy-done.4
  2.5 0.8 copy-done.6
  3.3 3.8 %shard_map.163 = (f32[2048,128]{1,0:T(8,128)S(1)}, bf16[4096,256]{1,0:T(8,128)(2,1)S(1)}) custom-call(bf16[64,64,128]{2,1,0:T(8,128)(2,1)S(1)} %bitcast.25, bf16[64,64,128]{2,1,0:T(8,128)(2,1)S(1)} %bitcast.26, bf16[128,256]{1,0:T(8,128)(2,1)S(1)} %copy-done.6), custom_call_target="tpu_custom_call" | custom-call | tf_op jit(solution)/shard_map/pallas_call | solution.py:314
  7.1 36.6 %all_to_all.25 = f32[32,64,128]{2,1,0:T(8,128)S(1)} all-to-all(f32[32,64,128]{2,1,0:T(8,128)S(1)} %bitcast.27), channel_id=1, replica_groups=mesh['grp'=8,'slab'=32] {'slab'}, dimensions={0} | all-to-all | bytes 2097152 | tf_op jit(solution)/shard_map/all_to_all | solution.py:285
  43.7 0.6 shard_map.164
  44.3 15.6 %all_to_all.26 = f32[8,64,128]{2,1,0:T(8,128)S(1)} all-to-all(f32[8,64,128]{2,1,0:T(8,128)S(1)} %bitcast.28), channel_id=1, replica_groups=mesh['grp'=8,'slab'=32] {'grp'}, dimensions={0} | all-to-all | bytes 524288 | tf_op jit(solution)/shard_map/all_to_all | solution.py:285
  59.9 2.2 %shard_map.165 = f32[512,128]{1,0:T(8,128)S(1)} custom-call(f32[512,128]{1,0:T(8,128)S(1)} %bitcast.30, bf16[8192,128]{1,0:T(8,128)(2,1)S(1)} %bitcast.24, bf16[128,256]{1,0:T(8,128)(2,1)S(1)} %copy-done.6, bf16[128,192]{1,0:T(8,128)(2,1)S(1)} %copy-done.5), custom_call_target="tpu_custom_call" | custom-call | tf_op jit(solution)/shard_map/pallas_call | solution.py:359
  62.1 10.1 %all_to_all.27 = f32[8,64,128]{2,1,0:T(8,128)S(1)} all-to-all(f32[8,64,128]{2,1,0:T(8,128)S(1)} %bitcast.31), channel_id=1, replica_groups=mesh['grp'=8,'slab'=32] {'grp'}, dimensions={0} | all-to-all | bytes 524288 | tf_op jit(solution)/shard_map/all_to_all | solution.py:285
  72.2 1.6 %shard_map.166 = f32[2048,128]{1,0:T(8,128)} custom-call(f32[512,128]{1,0:T(8,128)S(1)} %bitcast.29, bf16[128,192]{1,0:T(8,128)(2,1)S(1)} %copy-done.5), custom_call_target="tpu_custom_call" | custom-call | tf_op jit(solution)/shard_map/pallas_call | solution.py:363
  73.8 4.9 %all-to-all-start.3 = ((f32[32,64,128]{2,1,0:T(8,128)}), f32[32,64,128]{2,1,0:T(8,128)S(1)}, u32[]{:S(2)}, u32[]{:S(2)}) async-start(f32[32,64,128]{2,1,0:T(8,128)} %bitcast.9), calls=%async_computation.3 | async-start | bytes 2097152 | tf_op jit(solution)/shard_map/all_to_all | solution.py:285
  78.8 0.1 pad.13.clone
  78.9 1.1 shard_map.169
  80.0 0.1 maximum_maximum_fusion.1.weight_ref
  80.1 6.1 %shard_map.168.local_ref = f32[1024,128]{1,0:T(8,128)S(1)} custom-call(bf16[4096,256]{1,0:T(8,128)(2,1)S(1)} %get-tuple-element.16.grad_ref, bf16[128,128]{1,0:T(8,128)(2,1)S(1)} %maximum_maximum_fusion.1.weight_ref, s32[1024]{0:T(1024)S(1)} %copy-done.8), custom_call_target="tpu_custom_call" | custom-call | tf_op jit(solution)/shard_map/pallas_call | solution.py:349
  86.3 0.8 copy-done.1
  87.3 4.5 %shard_map.167.kernel_ref = f32[1024,128]{1,0:T(8,128)S(1)} custom-call(f32[8,1024]{1,0:T(8,128)S(1)} %maximum_maximum_fusion.in_ref, f32[8,512]{1,0:T(8,128)S(1)} %maximum_maximum_fusion.2.w_in_ref, f32[512,256]{1,0:T(8,128)S(1)} %copy-done.7, f32[1,256]{1,0:T(1,128)S(1)} %bitcast.35, f32[128,256]{1,0:T(8,128)S(1)} %pad_maximum_fusion.w_out_ref, ...), custom_call_target="tpu_custom_call" | custom-call | tf_op jit(solution)/shard_map/pallas_call | solution.py:336
  91.9 11.7 %all-to-all-done.3 = f32[32,64,128]{2,1,0:T(8,128)S(1)} async-done(((f32[32,64,128]{2,1,0:T(8,128)}), f32[32,64,128]{2,1,0:T(8,128)S(1)}, u32[]{:S(2)}, u32[]{:S(2)}) %all-to-all-start.3) | async-done | bytes 1048608 | tf_op jit(solution)/shard_map/all_to_all | solution.py:285
  103.5 1.0 copy-done.2
  104.6 5.6 %shard_map.170 = f32[1280,128]{1,0:T(8,128)S(1)} custom-call(f32[2048,128]{1,0:T(8,128)S(1)} %bitcast.22, bf16[128,192]{1,0:T(8,128)(2,1)S(1)} %copy-done.5, f32[1024,128]{1,0:T(8,128)S(1)} %shard_map.167.kernel_ref, f32[1024,128]{1,0:T(8,128)S(1)} %copy-done.2, f32[256,128]{1,0:T(8,128)S(1)} %get-tuple-element.19.targets_ref, s32[1024]{0:T(1024)S(1)} %bitcast.32, ...), custom_call_target="tpu_custom_call" | custom-call | tf_op jit(solution)/shard_map/pallas_call | solution.py:365
  110.2 0.1 reshape.62
  110.3 42.8 %all_to_all.28 = f32[256,5,128]{2,1,0:T(8,128)S(1)} all-to-all(f32[256,5,128]{2,1,0:T(8,128)S(1)} %reshape.62), channel_id=1, replica_groups=mesh['grp'=8,'slab'=32] {'grp','slab'}, dimensions={0} | all-to-all | bytes 1310720 | tf_op jit(solution)/shard_map/all_to_all | solution.py:285
  153.1 0.1 reshape.63.in_ref
  153.2 1.6 %shard_map.171 = f32[64,1024]{1,0:T(8,128)} custom-call(f32[1280,128]{1,0:T(8,128)S(1)} %reshape.63.in_ref), custom_call_target="tpu_custom_call" | custom-call | tf_op jit(solution)/shard_map/pallas_call | solution.py:372
  (38 shorter events, 0.4 us)
Async XLA Ops:
  0.0 1.2 copy-start.3
  1.2 1.2 copy-start.4
  2.5 0.8 copy-start.6
  7.1 52.8 %copy-start = (bf16[1,4,32,64,128]{4,3,2,1,0:T(8,128)(2,1)S(1)}, bf16[1,4,32,64,128]{4,3,2,1,0:T(8,128)(2,1)}, u32[]{:S(2)}) copy-start(bf16[1,4,32,64,128]{4,3,2,1,0:T(8,128)(2,1)} %param.20) | copy-start | bytes 6291460
  7.1 52.8 %copy-start.5 = (bf16[128,192]{1,0:T(8,128)(2,1)S(1)}, bf16[128,192]{1,0:T(8,128)(2,1)}, u32[]{:S(2)}) copy-start(bf16[128,192]{1,0:T(8,128)(2,1)} %constant.10.clone.inverse_ref.table_ref) | copy-start | bytes 147460
  62.1 16.8 %copy-start.9 = (s32[1024,1]{0,1:T(1,128)S(1)}, s32[1024,1]{0,1:T(1,128)}, u32[]{:S(2)}) copy-start(s32[1024,1]{0,1:T(1,128)} %param.29) | copy-start | bytes 12292
  62.1 16.8 %copy-start.10 = (s32[1024]{0:T(1024)S(1)}, s32[1024]{0:T(1024)}, u32[]{:S(2)}) copy-start(s32[1024]{0:T(1024)} %param.30) | copy-start | bytes 12292
  62.1 17.9 %copy-start.15 = (bf16[64,64]{1,0:T(8,128)(2,1)S(1)}, bf16[64,64]{1,0:T(8,128)(2,1)}, u32[]{:S(2)}) copy-start(bf16[64,64]{1,0:T(8,128)(2,1)} %param.19) | copy-start | bytes 24580
  62.1 18.0 %copy-start.8 = (s32[1024]{0:T(1024)S(1)}, s32[1024]{0:T(1024)}, u32[]{:S(2)}) copy-start(s32[1024]{0:T(1024)} %voxel_ref.3) | copy-start | bytes 12292
  73.7 13.3 %copy-start.18 = (f32[64]{0:T(128)S(1)}, f32[64]{0:T(128)}, u32[]{:S(2)}) copy-start(f32[64]{0:T(128)} %param.26) | copy-start | bytes 772
  73.7 13.4 %copy-start.13 = (f32[256,64]{0,1:T(8,128)S(1)}, f32[256,64]{0,1:T(8,128)}, u32[]{:S(2)}) copy-start(f32[256,64]{0,1:T(8,128)} %param.25) | copy-start | bytes 196612
  73.8 13.4 %copy-start.16 = (f32[6,512]{1,0:T(8,128)S(1)}, f32[6,512]{1,0:T(8,128)}, u32[]{:S(2)}) copy-start(f32[6,512]{1,0:T(8,128)} %param.21) | copy-start | bytes 36868
  73.8 13.4 %copy-start.17 = (f32[512]{0:T(512)S(1)}, f32[512]{0:T(512)}, u32[]{:S(2)}) copy-start(f32[512]{0:T(512)} %param.22) | copy-start | bytes 6148
  73.8 13.5 %copy-start.14 = (f32[6,1024]{1,0:T(8,128)S(1)}, f32[6,1024]{1,0:T(8,128)}, u32[]{:S(2)}) copy-start(f32[6,1024]{1,0:T(8,128)} %param.27) | copy-start | bytes 73732
  73.8 13.6 %copy-start.11 = (f32[256]{0:T(256)S(1)}, f32[256]{0:T(256)}, u32[]{:S(2)}) copy-start(f32[256]{0:T(256)} %param.24) | copy-start | bytes 3076
  73.8 13.5 %copy-start.12 = (s32[8]{0:T(128)S(1)}, s32[8]{0:T(128)}, u32[]{:S(2)}) copy-start(s32[8]{0:T(128)} %counts_ref.1) | copy-start | bytes 100
  73.8 29.7 %all-to-all-start.3 = ((f32[32,64,128]{2,1,0:T(8,128)}), f32[32,64,128]{2,1,0:T(8,128)S(1)}, u32[]{:S(2)}, u32[]{:S(2)}) async-start(f32[32,64,128]{2,1,0:T(8,128)} %bitcast.9), calls=%async_computation.3 | async-start | bytes 2097152 | tf_op jit(solution)/shard_map/all_to_all | solution.py:285
  78.7 8.6 %copy-start.7 = (f32[512,256]{1,0:T(8,128)S(1)}, f32[512,256]{1,0:T(8,128)}, u32[]{:S(2)}) copy-start(f32[512,256]{1,0:T(8,128)} %w_mid_ref.1) | copy-start | bytes 1572868
  86.3 0.8 copy-start.1
  103.5 1.0 copy-start.2
where the time goes:
time: 155 us
  blocking collectives  105 us (68%)
  Pallas kernels  27.1 us (17%)
  waiting for transfers between devices  11.7 us (8%)
  local copies, waits for them, and re-layouts  5.53 us (4%)
  starting transfers between devices  4.94 us (3%)
    all_to_all x4, blocking collectives, exchange(): lax.all_to_all(rows.reshape(members, count, 128), axis, split_axis=0, con...  105 us
    all_to_all x1, waiting for transfers between devices, exchange(): lax.all_to_all(rows.reshape(members, count, 128), axis, split_axis=0, con...  11.7 us
    pallas_call x1, Pallas kernels, local(): call(local_kernel, shape((1024, 128), F32), [VMEM, VMEM, SMEM], [pltpu.VM...  6.13 us
    pallas_call x1, Pallas kernels, local(): call(slots_kernel, shape((1280, 128), F32), [VMEM] * 5 + [SMEM] * 2, [plt...  5.63 us
    unnamed x38, local copies, waits for them, and re-layouts  5.19 us
    all_to_all x1, starting transfers between devices, exchange(): lax.all_to_all(rows.reshape(members, count, 128), axis, split_axis=0, con...  4.94 us
    pallas_call x1, Pallas kernels, local(): call(kernel_net_kernel, shape((1024, 128), F32), [VMEM] * 6 + [SMEM])  4.53 us
    pallas_call x1, Pallas kernels, local(): call(modes_z_kernel, (shape((2048, 128), F32), shape((4096, 256), BF16)),...  3.77 us
  transfers between devices with their start and end apart: 1, of which 1 were waited for; matrix products, arithmetic and copies ran while one was open for 0% of the time, Pallas kernels for 8%

commit v1 on v0

--- a/solution.py
+++ b/solution.py
@@ -67,23 +67,85 @@
     return cos_part, sin_part
 
 
-def modes_z_kernel(pre_ref, cotan_ref, table_ref, out_ref, grad_ref):
-    step = pl.program_id(0)
-    pre = pre_ref[...].astype(F32).reshape(512, 128)
-    cotan = cotan_ref[...].astype(F32).reshape(512, 128)
+def slope_times(pre, cotan):
     cdf = 0.5 * (1.0 + lax.erf(pre * (1.0 / math.sqrt(2.0))))
-    grad = cotan * (cdf + pre * jnp.exp(-0.5 * pre * pre) * (1.0 / math.sqrt(2.0 * math.pi)))
-    high, low = split(grad)
-    both = jnp.concatenate([high, low], axis=1)
-    grad_ref[...] = both
-    product = dot(table_ref[...], both, NT)
-    for pair in range(4):
-        real, minus = forward_parts(product, pair * 128, 128)
-        imag = -minus
-        left = lanes_of(real.shape) < 64
-        row = step * 8 + 2 * pair
-        out_ref[pl.ds(row, 32, stride=64), :] = jnp.where(left, real, swap(imag))
-        out_ref[pl.ds(row + 1, 32, stride=64), :] = jnp.where(left, swap(real), imag)
+    return cotan * (cdf + pre * jnp.exp(-0.5 * pre * pre) * (1.0 / math.sqrt(2.0 * math.pi)))
+
+
+def rank_slots(dest, target, code_ref, send_ref):
+    hit = lax.broadcasted_iota(jnp.int32, (256, 1024), 0) == dest
+    one_hot = jnp.where(hit, 1.0, 0.0).astype(BF16)
+    lane = lanes_of((128, 256))
+    earlier = (lax.broadcasted_iota(jnp.int32, (128, 256), 0) < lane) | (lane >= 128)
+    earlier = jnp.where(earlier, 1.0, 0.0).astype(BF16)
+    before = jnp.zeros((256, 128), F32)
+    ranks = []
+    for block in range(8):
+        at = slice(block * 128, block * 128 + 128)
+        count = dot(one_hot[:, at], earlier)
+        own = jnp.where(hit[:, at], count[:, :128] + before, 0.0)
+        ranks.append(jnp.sum(own, axis=0, keepdims=True))
+        before = before + count[:, 128:]
+    rank = jnp.concatenate(ranks, axis=1).astype(jnp.int32)
+    code_ref[...] = dest * 8 + rank
+    number = target + 1
+    group = lax.broadcasted_iota(jnp.int32, (16, 1024), 0) == (dest >> 5)
+    group = jnp.where(group, 1.0, 0.0).astype(BF16)
+    own = lax.broadcasted_iota(jnp.int32, (256, 1024), 0) == ((dest & 31) * 8 + rank)
+    coarse = jnp.where(own, ((number >> 5) << 5).astype(F32), 0.0).astype(BF16)
+    fine = jnp.where(own, (number & 31).astype(F32), 0.0).astype(BF16)
+    send_ref[...] = (dot(group, coarse, NT) + dot(group, fine, NT))[:8]
+
+
+def modes_z_kernel(
+    pre_hbm,
+    cotan_hbm,
+    table_hbm,
+    dest_hbm,
+    target_hbm,
+    out_ref,
+    code_ref,
+    send_ref,
+    pre_ref,
+    cotan_ref,
+    table_ref,
+    dest_ref,
+    target_ref,
+    sems,
+    small_sems,
+):
+    small = (
+        pltpu.make_async_copy(dest_hbm, dest_ref, small_sems.at[0]),
+        pltpu.make_async_copy(target_hbm, target_ref, small_sems.at[1]),
+        pltpu.make_async_copy(table_hbm, table_ref, small_sems.at[2]),
+    )
+    for copy in small:
+        copy.start()
+    loads = []
+    for step in range(8):
+        at = pl.ds(step * 8, 8)
+        loads.append(pltpu.make_async_copy(pre_hbm.at[at], pre_ref.at[at], sems.at[step, 0]))
+        loads.append(pltpu.make_async_copy(cotan_hbm.at[at], cotan_ref.at[at], sems.at[step, 1]))
+    for copy in loads:
+        copy.start()
+    for copy in small:
+        copy.wait()
+    rank_slots(dest_ref[...], target_ref[...], code_ref, send_ref)
+    for copy in loads:
+        copy.wait()
+    for step in range(8):
+        at = pl.ds(step * 8, 8)
+        pre = pre_ref[at].astype(F32).reshape(512, 128)
+        cotan = cotan_ref[at].astype(F32).reshape(512, 128)
+        high, low = split(slope_times(pre, cotan))
+        product = dot(table_ref[...], jnp.concatenate([high, low], axis=1), NT)
+        for pair in range(4):
+            real, minus = forward_parts(product, pair * 128, 128)
+            imag = -minus
+            left = lanes_of(real.shape) < 64
+            row = step * 8 + 2 * pair
+            out_ref[pl.ds(row, 32, stride=64), :] = jnp.where(left, real, swap(imag))
+            out_ref[pl.ds(row + 1, 32, stride=64), :] = jnp.where(left, swap(real), imag)
 
 
 def modes_x_kernel(in_ref, table_ref, out_ref):
@@ -102,7 +164,9 @@
     return jnp.concatenate([mixed_high, mixed_low, mixed_high, high, low, high], axis=0)
 
 
-def mix_kernel(in_ref, spectral_ref, forward_ref, inverse_ref, out_ref):
+def mix_kernel(in_ref, spectral_ref, forward_ref, inverse_ref, targets_ref, out_ref):
+    for half in range(2):
+        out_ref[pl.ds(64 + half, 8, stride=66), :] = targets_ref[:, half * 128 : half * 128 + 128]
     for kx in range(4):
         data = jnp.concatenate(
             [in_ref[g * 64 + kx * 16 : g * 64 + kx * 16 + 16, :] for g in range(8)], axis=0
@@ -141,37 +205,41 @@
         mixed = jnp.concatenate(halves, axis=0) * (1.0 / float(NG) ** 3)
         field = dot(inverse_ref[...], inverse_stack(mixed))
         for g in range(8):
-            out_ref[g * 64 + kx * 16 : g * 64 + kx * 16 + 16, :] = field[g * 16 : g * 16 + 16]
+            out_ref[g * 66 + kx * 16 : g * 66 + kx * 16 + 16, :] = field[g * 16 : g * 16 + 16]
 
 
 def field_x_kernel(in_ref, table_ref, out_ref):
+    number = jnp.concatenate(
+        [in_ref[pl.ds(64 + half, 8, stride=66), :] for half in range(2)], axis=1
+    ).astype(jnp.int32)
+    own = (lanes_of((32, 256)) >> 3) == lax.broadcasted_iota(jnp.int32, (32, 256), 0)
+    total = jnp.zeros((64, 128), F32)
+    for g in range(8):
+        row = number[g : g + 1]
+        coarse = jnp.where(own, ((row >> 5) << 5).astype(F32), 0.0)
+        fine = jnp.where(own, (row & 31).astype(F32), 0.0)
+        place = (lax.broadcasted_iota(jnp.int32, (256, 128), 0) & 7) + g * 8
+        fold = jnp.where(place == lanes_of((256, 128)), 1.0, 0.0).astype(BF16)
+        total = total + dot(jnp.concatenate([coarse, fine], axis=0).astype(BF16), fold)
+    out_ref[pl.ds(64, 32, stride=65), :] = total[:32] + total[32:]
     for y in range(0, 16, 2):
-        stack = jnp.concatenate(
-            [inverse_stack(in_ref[pl.ds(y + h, 32, stride=16), :]) for h in range(2)], axis=1
-        )
-        field = dot(table_ref[...], stack)
+        stacks = []
         for h in range(2):
-            out_ref[pl.ds(y + h, 128, stride=16), :] = field[:, h * 128 : h * 128 + 128]
-
-
-def rank_kernel(dest_ref, target_ref, code_ref, send_ref):
-    dest = dest_ref[...]
-    hit = lax.broadcasted_iota(jnp.int32, (256, 1024), 0) == dest
-    one_hot = jnp.where(hit, 1.0, 0.0).astype(BF16)
-    earlier = lax.broadcasted_iota(jnp.int32, (1024, 1024), 0) < lanes_of((1024, 1024))
-    count = dot(one_hot, jnp.where(earlier, 1.0, 0.0).astype(BF16))
-    rank = jnp.sum(jnp.where(hit, count, 0.0), axis=0, keepdims=True).astype(jnp.int32)
-    code_ref[...] = (dest * 5 + (rank >> 1)) * 2 + (rank & 1)
-    number = target_ref[...] + 1
-    own = lax.broadcasted_iota(jnp.int32, (128, 1024), 0) == rank
-    coarse = jnp.where(own, ((number >> 5) << 5).astype(F32), 0.0).astype(BF16)
-    fine = jnp.where(own, (number & 31).astype(F32), 0.0).astype(BF16)
-    send_ref[...] = dot(one_hot, coarse, NT) + dot(one_hot, fine, NT) - 1.0
+            low = in_ref[pl.ds(y + h, 4, stride=16), :]
+            parts = [low] + [in_ref[pl.ds(g * 66 + y + h, 4, stride=16), :] for g in range(1, 8)]
+            stacks.append(inverse_stack(jnp.concatenate(parts, axis=0)))
+        field = dot(table_ref[...], jnp.concatenate(stacks, axis=1))
+        for h in range(2):
+            for s in range(32):
+                out_ref[pl.ds(s * 65 + y + h, 4, stride=16), :] = field[
+                    s * 4 : s * 4 + 4, h * 128 : h * 128 + 128
+                ]
 
 
 def kernel_net_kernel(
-    in_ref, w_in_ref, w_mid_ref, b_mid_ref, w_out_ref, b_out_ref, counts_ref, out_ref
+    in_ref, w_in_ref, w_mid_ref, b_mid_ref, w_out_ref, b_out_ref, counts_ref, after_hbm, out_ref
 ):
+    del after_hbm
     high = lax.Precision.HIGH
     for block in range(4):
         at = slice(block * 256, block * 256 + 256)
@@ -185,14 +253,19 @@
             )
 
 
-def local_kernel(grad_ref, weight_ref, voxel_ref, out_ref, table_ref):
+def local_kernel(pre_ref, cotan_ref, weight_ref, voxel_ref, after_hbm, out_ref, table_ref):
+    del after_hbm
+
     def fill(step, carry):
+        at = pl.ds(step * 4, 4)
+        pre = pre_ref[at].astype(F32).reshape(256, 128)
+        cotan = cotan_ref[at].astype(F32).reshape(256, 128)
+        high, low = split(slope_times(pre, cotan))
         for part in range(4):
-            cell = step * 4 + part
-            grad = grad_ref[pl.ds(pl.multiple_of(cell * 64, 64), 64), :]
-            stack = jnp.concatenate([grad[:, :128], grad[:, 128:]], axis=0)
-            rows = dot(weight_ref[...], stack)
-            table_ref[pl.ds(pl.multiple_of(cell * 128, 128), 128), :] = rows.T
+            own = slice(part * 64, part * 64 + 64)
+            rows = dot(weight_ref[...], jnp.concatenate([high[own], low[own]], axis=0))
+            first = pl.multiple_of((step * 4 + part) * 128, 128)
+            table_ref[pl.ds(first, 128), :] = rows.T
         return carry
 
     lax.fori_loop(0, 16, fill, 0)
@@ -207,17 +280,34 @@
 
 
 def slots_kernel(
-    in_ref, table_ref, kernel_ref, local_ref, targets_ref, code_ref, voxel_ref, out_ref, field_ref
+    in_ref,
+    table_ref,
+    kernel_hbm,
+    local_hbm,
+    code_ref,
+    voxel_ref,
+    out_ref,
+    numbers_ref,
+    field_ref,
+    kernel_ref,
+    local_ref,
+    sems,
 ):
+    copies = (
+        pltpu.make_async_copy(kernel_hbm, kernel_ref, sems.at[0]),
+        pltpu.make_async_copy(local_hbm, local_ref, sems.at[1]),
+    )
+    for copy in copies:
+        copy.start()
     out_ref[...] = jnp.zeros_like(out_ref)
-    out_ref[pl.ds(4, 256, stride=5), :] = targets_ref[...]
+    numbers_ref[...] = in_ref[pl.ds(64, 32, stride=65), :]
 
     def fill(step, carry):
         for part in range(4):
             stacks = []
             first = step * 8 + part * 2
             for h in range(2):
-                data = in_ref[pl.ds(first + h, 32, stride=64), :]
+                data = in_ref[pl.ds(first + h, 32, stride=65), :]
                 other = swap(data)
                 left = lanes_of(data.shape) < 64
                 real_high, real_low = split(jnp.where(left, data, other))
@@ -233,8 +323,10 @@
                 field_ref[pl.ds(at, 128), :] = field[:, h * 128 : h * 128 + 128]
         return carry
 
-    lax.fori_loop(0, 8, fill, 0)
+    lax.fori_loop(0, 8, fill, 0, unroll=2)
     side = lanes_of((1, 128)) >> 6
+    for copy in copies:
+        copy.wait()
 
     def place(step, carry):
         for part in range(16):
@@ -246,19 +338,22 @@
             pltpu.store(out_ref.at[pl.ds(code >> 1, 1), :], value, mask=side == (code & 1))
         return carry
 
-    lax.fori_loop(0, 64, place, 0)
-
-
-def gather_kernel(in_ref, out_ref):
-    targets = in_ref[pl.ds(4, 256, stride=5), :]
+    lax.fori_loop(0, 64, place, 0, unroll=2)
+
+
+def gather_kernel(in_ref, numbers_ref, out_ref):
+    numbers = numbers_ref[...] - 1.0
     point = lanes_of((256, 1024)).astype(F32)
     total = jnp.zeros((128, 1024), F32)
     for pair in range(4):
-        data = in_ref[pl.ds(pair, 256, stride=5), :].T
+        data = in_ref[pl.ds(pair, 256, stride=4), :].T
         high, low = split(data)
         for h in range(2):
             at = slice(h * 64, h * 64 + 64)
-            column = targets[:, pair * 2 + h : pair * 2 + h + 1]
+            rank = pair * 2 + h
+            column = jnp.concatenate(
+                [numbers[:, g * 8 + rank : g * 8 + rank + 1] for g in range(8)], axis=0
+            )
             one_hot = jnp.where(column == point, 1.0, 0.0).astype(BF16)
             total = total + dot(jnp.concatenate([high[at], low[at]], axis=0), one_hot)
     out_ref[...] = total[:64] + total[64:]
@@ -266,7 +361,9 @@
 
 VMEM = pl.BlockSpec(memory_space=pltpu.VMEM)
 SMEM = pl.BlockSpec(memory_space=pltpu.SMEM)
-LIMIT = 48 * 1024 * 1024
+HBM = pl.BlockSpec(memory_space=pltpu.HBM)
+ANY = pl.BlockSpec(memory_space=pl.ANY)
+LIMIT = 16 * 1024 * 1024
 
 
 def call(body, out_shape, in_specs, scratch=(), **more):
@@ -280,11 +377,14 @@
     )
 
 
+def in_hbm(x):
+    return pltpu.with_memory_space_constraint(x, pltpu.HBM)
+
+
 def exchange(rows, axis, members):
     count = rows.shape[0] // members
-    moved = lax.all_to_all(
-        rows.reshape(members, count, 128), axis, split_axis=0, concat_axis=0, tiled=True
-    )
+    chunks = (members, count, 128) if count % 8 == 0 else (members, 1, count * 128)
+    moved = lax.all_to_all(rows.reshape(chunks), axis, split_axis=0, concat_axis=0, tiled=True)
     return moved.reshape(rows.shape)
 
 
@@ -308,33 +408,43 @@
     forward, inverse = tables()
     forward, inverse = jnp.asarray(forward), jnp.asarray(inverse)
     shape = jax.ShapeDtypeStruct
-
-    block = pl.BlockSpec((8, 64, 128), lambda i: (i, 0, 0))
-    whole = pl.BlockSpec((128, 256), lambda i: (0, 0))
-    columns, grad = call(
+    pre, cotan = pre.reshape(64, 64, 128), cotan.reshape(64, 64, 128)
+
+    columns, code, send_targets = call(
         modes_z_kernel,
-        (shape((2048, 128), F32), shape((4096, 256), BF16)),
-        [block, block, whole],
-        grid=(8,),
-        out_specs=(
-            pl.BlockSpec((2048, 128), lambda i: (0, 0)),
-            pl.BlockSpec((512, 256), lambda i: (i, 0)),
-        ),
-    )(pre.reshape(64, 64, 128), cotan.reshape(64, 64, 128), forward)
-
-    routes, targets, kernel_inputs, grad = lax.optimization_barrier(
-        (routes, targets, kernel_inputs, grad)
-    )
-    code, send_targets = call(
-        rank_kernel,
-        (shape((1, 1024), jnp.int32), shape((256, 128), F32)),
-        [VMEM, VMEM],
-    )(routes.reshape(1, 1024), targets.reshape(1, 1024))
+        (shape((2048, 128), F32), shape((1, 1024), jnp.int32), shape((8, 256), F32)),
+        [HBM] * 5,
+        [
+            pltpu.VMEM((64, 64, 128), BF16),
+            pltpu.VMEM((64, 64, 128), BF16),
+            pltpu.VMEM((128, 256), BF16),
+            pltpu.VMEM((1, 1024), jnp.int32),
+            pltpu.VMEM((1, 1024), jnp.int32),
+            pltpu.SemaphoreType.DMA((8, 2)),
+            pltpu.SemaphoreType.DMA((3,)),
+        ],
+    )(
+        in_hbm(pre),
+        in_hbm(cotan),
+        in_hbm(forward),
+        in_hbm(routes.reshape(1, 1024)),
+        in_hbm(targets.reshape(1, 1024)),
+    )
     code = code.reshape(1024)
+
+    columns = exchange(columns, "slab", 32)
+    rows = call(modes_x_kernel, shape((512, 128), F32), [VMEM, VMEM])(columns, forward)
+    rows = exchange(rows, "grp", 8)
+    rows = call(mix_kernel, shape((528, 128), F32), [VMEM] * 5)(
+        rows, spectral.reshape(8192, 128), forward, inverse, send_targets
+    )
+    rows = exchange(rows, "grp", 8)
+    columns = call(field_x_kernel, shape((2080, 128), F32), [VMEM, VMEM])(rows, inverse)
+
     net_in = jnp.concatenate([kernel_inputs, jnp.ones((1, 1024), F32), jnp.zeros((1, 1024), F32)])
     first_layer = jnp.concatenate([w_in, b_in[None], jnp.zeros((1, 512), F32)])
     kernel = call(
-        kernel_net_kernel, shape((1024, 128), F32), [VMEM] * 6 + [SMEM]
+        kernel_net_kernel, pltpu.HBM((1024, 128), F32), [VMEM] * 6 + [SMEM, ANY]
     )(
         net_in,
         first_layer,
@@ -343,33 +453,31 @@
         jnp.concatenate([w_out.T, w_out.T]),
         jnp.concatenate([b_out, b_out])[None],
         counts,
+        columns,
     )
     weight = jnp.concatenate([pointwise, pointwise], axis=0)
     weight = jnp.concatenate([weight, weight], axis=1)
     own = call(
         local_kernel,
-        shape((1024, 128), F32),
-        [VMEM, VMEM, SMEM],
+        pltpu.HBM((1024, 128), F32),
+        [VMEM, VMEM, VMEM, SMEM, ANY],
         [pltpu.VMEM((8192, 128), F32)],
-    )(grad, weight, voxel_index)
+    )(pre, cotan, weight, voxel_index, columns)
 
     columns = exchange(columns, "slab", 32)
-    rows = call(modes_x_kernel, shape((512, 128), F32), [VMEM, VMEM])(columns, forward)
-    rows = exchange(rows, "grp", 8)
-    rows = call(mix_kernel, shape((512, 128), F32), [VMEM] * 4)(
-        rows, spectral.reshape(8192, 128), forward, inverse
-    )
-    rows = exchange(rows, "grp", 8)
-    columns = call(field_x_kernel, shape((2048, 128), F32), [VMEM, VMEM])(rows, inverse)
-    columns = exchange(columns, "slab", 32)
-    slots = call(
+    slots, numbers = call(
         slots_kernel,
-        shape((1280, 128), F32),
-        [VMEM] * 5 + [SMEM] * 2,
-        [pltpu.VMEM((8192, 128), F32)],
-    )(columns, inverse, kernel, own, send_targets, code, voxel_index)
+        (shape((1024, 128), F32), shape((32, 128), F32)),
+        [VMEM, VMEM, HBM, HBM, SMEM, SMEM],
+        [
+            pltpu.VMEM((8192, 128), F32),
+            pltpu.VMEM((1024, 128), F32),
+            pltpu.VMEM((1024, 128), F32),
+            pltpu.SemaphoreType.DMA((2,)),
+        ],
+    )(columns, inverse, in_hbm(kernel), in_hbm(own), code, voxel_index)
     slots = exchange(slots, ("grp", "slab"), 256)
-    return call(gather_kernel, shape((64, 1024), F32), [VMEM])(slots)
+    return call(gather_kernel, shape((64, 1024), F32), [VMEM, VMEM])(slots, numbers)
 
 
 def solution(mesh):

time: 155 us -> 141 us (0.910)
  blocking collectives: 105 us -> 94.3 us
  local copies, waits for them, and re-layouts: 5.53 us -> 0.23 us
    all_to_all x4, blocking collectives: 105 us -> 94.3 us  [exchange(): lax.all_to_all(rows.reshape(chunks), axis, split_axis=0, concat_axis=0, t...]
    unnamed x38 -> x30, local copies, waits for them, and re-layouts: 5.19 us -> 0.08 us
    pallas_call x8 -> x7, Pallas kernels: 26.5 us -> 27.6 us  [the longest x1 7.52 us: local(): call(local_kernel, pltpu.HBM((1024, 128), F32), [VMEM, VMEM, VMEM, SMEM,...]
  transfers between devices with their start and end apart: 1 -> 1, of which waited for: 1 -> 1; matrix products, arithmetic and copies ran while one was open for 0% -> 0% of each run, Pallas kernels for 8% -> 9%
where the time goes in v1:
time: 141 us; the launch traced here: 140 us
  blocking collectives  94.3 us (67%)
  Pallas kernels  28.2 us (20%)
  waiting for transfers between devices  12.1 us (9%)
  starting transfers between devices  4.94 us (4%)
    all_to_all x4, blocking collectives, exchange(): lax.all_to_all(rows.reshape(chunks), axis, split_axis=0, concat_axis=0, t...  94.3 us
    all_to_all x1, waiting for transfers between devices, exchange(): lax.all_to_all(rows.reshape(chunks), axis, split_axis=0, concat_axis=0, t...  12.1 us
    pallas_call x1, Pallas kernels, local(): call(local_kernel, pltpu.HBM((1024, 128), F32), [VMEM, VMEM, VMEM, SMEM,...  7.52 us
    pallas_call x1, Pallas kernels, local(): call(kernel_net_kernel, pltpu.HBM((1024, 128), F32), [VMEM] * 6 + [SMEM,...  5.35 us
    all_to_all x1, starting transfers between devices, exchange(): lax.all_to_all(rows.reshape(chunks), axis, split_axis=0, concat_axis=0, t...  4.94 us
    pallas_call x1, Pallas kernels, local(): call(modes_z_kernel, (shape((2048, 128), F32), shape((1, 1024), jnp.int32...  4.9 us
    pallas_call x1, Pallas kernels, local(): call(slots_kernel, (shape((1024, 128), F32), shape((32, 128), F32)), [VME...  4.32 us
  transfers between devices with their start and end apart: 1, of which 1 were waited for; matrix products, arithmetic and copies ran while one was open for 0% of the time, Pallas kernels for 9%

profile of v1, /device:TPU:1, one launch (start us, length us, event | category | flops | bytes accessed | tf_op | source)
XLA Modules:
  0.0 140.2 jit_solution(11941915135926823900)
XLA Ops:
  0.0 4.9 %shard_map.163 = (f32[2048,128]{1,0:T(8,128)S(1)}, s32[1,1024]{1,0:T(1,128)S(1)}, f32[8,256]{1,0:T(8,128)S(1)}) custom-call(bf16[64,64,128]{2,1,0:T(8,128)(2,1)} %bitcast.25, bf16[64,64,128]{2,1,0:T(8,128)(2,1)} %bitcast.27, bf16[128,256]{1,0:T(8,128)(2,1)} %constant.3.clone.table_hbm.table_ref.forward_ref, s32[1,1024]{1,0:T(1,128)} %bitcast.41, ...), custom_call_target="tpu_custom_call" | custom-call | tf_op jit(solution)/shard_map/pallas_call | solution.py:413
  4.9 0.0 copy-start.4
  4.9 0.0 copy-start.2
  4.9 36.6 %all_to_all.25 = f32[32,64,128]{2,1,0:T(8,128)S(1)} all-to-all(f32[32,64,128]{2,1,0:T(8,128)S(1)} %bitcast.34), channel_id=1, replica_groups=mesh['grp'=8,'slab'=32] {'slab'}, dimensions={0} | all-to-all | bytes 2097152 | tf_op jit(solution)/shard_map/all_to_all | solution.py:387
  41.5 0.6 shard_map.164
  42.2 15.6 %all_to_all.26 = f32[8,64,128]{2,1,0:T(8,128)S(1)} all-to-all(f32[8,64,128]{2,1,0:T(8,128)S(1)} %bitcast.35), channel_id=1, replica_groups=mesh['grp'=8,'slab'=32] {'grp'}, dimensions={0} | all-to-all | bytes 524288 | tf_op jit(solution)/shard_map/all_to_all | solution.py:387
  57.7 2.2 %shard_map.165 = f32[528,128]{1,0:T(8,128)S(1)} custom-call(f32[512,128]{1,0:T(8,128)S(1)} %bitcast.36, bf16[8192,128]{1,0:T(8,128)(2,1)S(1)} %bitcast.30, bf16[128,256]{1,0:T(8,128)(2,1)S(1)} %copy-done.4, bf16[128,192]{1,0:T(8,128)(2,1)S(1)} %copy-done.3, f32[8,256]{1,0:T(8,128)S(1)} %get-tuple-element.11.targets_ref), custom_call_target="tpu_custom_call" | custom-call | tf_op jit(solution)/shard_map/pallas_call | solution.py:438
  59.9 10.6 %all_to_all.27 = f32[8,1,8448]{2,1,0:T(1,128)S(1)} all-to-all(f32[8,1,8448]{2,1,0:T(1,128)S(1)} %bitcast.33), channel_id=1, replica_groups=mesh['grp'=8,'slab'=32] {'grp'}, dimensions={0} | all-to-all | bytes 540672 | tf_op jit(solution)/shard_map/all_to_all | solution.py:387
  70.5 1.6 %shard_map.166.after_hbm = f32[2080,128]{1,0:T(8,128)} custom-call(f32[528,128]{1,0:T(8,128)S(1)} %bitcast.32, bf16[128,192]{1,0:T(8,128)(2,1)S(1)} %copy-done.3), custom_call_target="tpu_custom_call" | custom-call | tf_op jit(solution)/shard_map/pallas_call | solution.py:442
  72.1 0.0 copy-start.1
  72.2 0.0 copy-start.6
  72.2 4.9 %all-to-all-start.3 = ((f32[32,1,8320]{2,1,0:T(1,128)}), f32[32,1,8320]{2,1,0:T(1,128)S(1)}, u32[]{:S(2)}, u32[]{:S(2)}) async-start(f32[32,1,8320]{2,1,0:T(1,128)} %bitcast.11), calls=%async_computation.3 | async-start | bytes 2129920 | tf_op jit(solution)/shard_map/all_to_all | solution.py:387
  77.1 0.1 pad.13.clone
  77.2 0.1 pad.12.clone
  77.3 0.1 maximum_bitcast_fusion.b_out_ref
  77.3 0.1 maximum_maximum_fusion.1.weight_ref
  77.5 0.1 maximum_maximum_fusion.2.w_in_ref
  77.6 0.1 maximum_maximum_fusion.in_ref
  77.7 7.5 %shard_map.168.local_hbm = f32[1024,128]{1,0:T(8,128)} custom-call(bf16[64,64,128]{2,1,0:T(8,128)(2,1)S(1)} %bitcast.26, bf16[64,64,128]{2,1,0:T(8,128)(2,1)S(1)} %bitcast.28, bf16[128,128]{1,0:T(8,128)(2,1)S(1)} %maximum_maximum_fusion.1.weight_ref, s32[1024]{0:T(1024)S(1)} %copy-done.6, f32[2080,128]{1,0:T(8,128)} %shard_map.166.after_hbm), custom_call_target="tpu_custom_call" | custom-call | tf_op jit(solution)/shard_map/pallas_call | solution.py:460
  85.2 5.3 %shard_map.167.kernel_hbm = f32[1024,128]{1,0:T(8,128)} custom-call(f32[8,1024]{1,0:T(8,128)S(1)} %maximum_maximum_fusion.in_ref, f32[8,512]{1,0:T(8,128)S(1)} %maximum_maximum_fusion.2.w_in_ref, f32[512,256]{1,0:T(8,128)S(1)} %copy-done.5, f32[1,256]{1,0:T(1,128)S(1)} %bitcast.39, f32[128,256]{1,0:T(8,128)S(1)} %pad_maximum_fusion.w_out_ref, ...), custom_call_target="tpu_custom_call" | custom-call | tf_op jit(solution)/shard_map/pallas_call | solution.py:446
  90.6 12.1 %all-to-all-done.3 = f32[32,1,8320]{2,1,0:T(1,128)S(1)} async-done(((f32[32,1,8320]{2,1,0:T(1,128)}), f32[32,1,8320]{2,1,0:T(1,128)S(1)}, u32[]{:S(2)}, u32[]{:S(2)}) %all-to-all-start.3) | async-done | bytes 1064992 | tf_op jit(solution)/shard_map/all_to_all | solution.py:387
  102.7 4.3 %shard_map.169 = (f32[1024,128]{1,0:T(8,128)S(1)}, f32[32,128]{1,0:T(8,128)S(1)}) custom-call(f32[2080,128]{1,0:T(8,128)S(1)} %bitcast.24, bf16[128,192]{1,0:T(8,128)(2,1)S(1)} %copy-done.3, f32[1024,128]{1,0:T(8,128)} %shard_map.167.kernel_hbm, f32[1024,128]{1,0:T(8,128)} %shard_map.168.local_hbm, s32[1024]{0:T(1024)S(1)} %bitcast.38, s32[1024]{0:T(1024)S(1)} %copy-done.6), custom_call_target="tpu_custom_call" | custom-call | tf_op jit(solution)/shard_map/pallas_call | solution.py:468
  107.0 31.5 %all_to_all.28 = f32[256,1,512]{2,1,0:T(1,128)S(1)} all-to-all(f32[256,1,512]{2,1,0:T(1,128)S(1)} %bitcast.37), channel_id=1, replica_groups=mesh['grp'=8,'slab'=32] {'grp','slab'}, dimensions={0} | all-to-all | bytes 1048576 | tf_op jit(solution)/shard_map/all_to_all | solution.py:387
  138.4 1.8 %shard_map.170 = f32[64,1024]{1,0:T(8,128)} custom-call(f32[1024,128]{1,0:T(8,128)S(1)} %bitcast.31, f32[32,128]{1,0:T(8,128)S(1)} %get-tuple-element.14.numbers_ref), custom_call_target="tpu_custom_call" | custom-call | tf_op jit(solution)/shard_map/pallas_call | solution.py:480
  (27 shorter events, 0.1 us)
Async XLA Ops:
  4.9 36.6 %copy-start.4 = (bf16[128,256]{1,0:T(8,128)(2,1)S(1)}, bf16[128,256]{1,0:T(8,128)(2,1)}, u32[]{:S(2)}) copy-start(bf16[128,256]{1,0:T(8,128)(2,1)} %constant.3.clone.table_hbm.table_ref.forward_ref) | copy-start | bytes 196612
  4.9 52.8 %copy-start.2 = (bf16[1,4,32,64,128]{4,3,2,1,0:T(8,128)(2,1)S(1)}, bf16[1,4,32,64,128]{4,3,2,1,0:T(8,128)(2,1)}, u32[]{:S(2)}) copy-start(bf16[1,4,32,64,128]{4,3,2,1,0:T(8,128)(2,1)} %param.20) | copy-start | bytes 6291460
  41.5 16.2 %copy-start.3 = (bf16[128,192]{1,0:T(8,128)(2,1)S(1)}, bf16[128,192]{1,0:T(8,128)(2,1)}, u32[]{:S(2)}) copy-start(bf16[128,192]{1,0:T(8,128)(2,1)} %constant.10.clone.inverse_ref.table_ref) | copy-start | bytes 147460
  70.5 6.7 %copy-start.14 = (f32[64]{0:T(128)S(1)}, f32[64]{0:T(128)}, u32[]{:S(2)}) copy-start(f32[64]{0:T(128)} %param.26) | copy-start | bytes 772
  70.5 6.8 %copy-start.11 = (bf16[64,64]{1,0:T(8,128)(2,1)S(1)}, bf16[64,64]{1,0:T(8,128)(2,1)}, u32[]{:S(2)}) copy-start(bf16[64,64]{1,0:T(8,128)(2,1)} %param.19) | copy-start | bytes 24580
  72.1 5.3 %copy-start.9 = (f32[256,64]{0,1:T(8,128)S(1)}, f32[256,64]{0,1:T(8,128)}, u32[]{:S(2)}) copy-start(f32[256,64]{0,1:T(8,128)} %param.25) | copy-start | bytes 196612
  72.1 5.3 %copy-start.12 = (f32[6,512]{1,0:T(8,128)S(1)}, f32[6,512]{1,0:T(8,128)}, u32[]{:S(2)}) copy-start(f32[6,512]{1,0:T(8,128)} %param.21) | copy-start | bytes 36868
  72.1 5.4 %copy-start.13 = (f32[512]{0:T(512)S(1)}, f32[512]{0:T(512)}, u32[]{:S(2)}) copy-start(f32[512]{0:T(512)} %param.22) | copy-start | bytes 6148
  72.1 5.4 %copy-start.10 = (f32[6,1024]{1,0:T(8,128)S(1)}, f32[6,1024]{1,0:T(8,128)}, u32[]{:S(2)}) copy-start(f32[6,1024]{1,0:T(8,128)} %param.27) | copy-start | bytes 73732
  72.1 5.5 %copy-start = (bf16[4,16,64,128]{3,2,1,0:T(8,128)(2,1)S(1)}, bf16[4,16,64,128]{3,2,1,0:T(8,128)(2,1)}, u32[]{:S(2)}) copy-start(bf16[4,16,64,128]{3,2,1,0:T(8,128)(2,1)} %param.17) | copy-start | bytes 3145732
  72.1 5.5 %copy-start.1 = (bf16[4,16,64,128]{3,2,1,0:T(8,128)(2,1)S(1)}, bf16[4,16,64,128]{3,2,1,0:T(8,128)(2,1)}, u32[]{:S(2)}) copy-start(bf16[4,16,64,128]{3,2,1,0:T(8,128)(2,1)} %param.18) | copy-start | bytes 3145732
  72.2 5.5 %copy-start.6 = (s32[1024]{0:T(1024)S(1)}, s32[1024]{0:T(1024)}, u32[]{:S(2)}) copy-start(s32[1024]{0:T(1024)} %voxel_ref.3) | copy-start | bytes 12292
  72.2 30.5 %all-to-all-start.3 = ((f32[32,1,8320]{2,1,0:T(1,128)}), f32[32,1,8320]{2,1,0:T(1,128)S(1)}, u32[]{:S(2)}, u32[]{:S(2)}) async-start(f32[32,1,8320]{2,1,0:T(1,128)} %bitcast.11), calls=%async_computation.3 | async-start | bytes 2129920 | tf_op jit(solution)/shard_map/all_to_all | solution.py:387
  77.7 7.6 %copy-start.5 = (f32[512,256]{1,0:T(8,128)S(1)}, f32[512,256]{1,0:T(8,128)}, u32[]{:S(2)}) copy-start(f32[512,256]{1,0:T(8,128)} %w_mid_ref.1) | copy-start | bytes 1572868
  77.7 7.6 %copy-start.7 = (f32[256]{0:T(256)S(1)}, f32[256]{0:T(256)}, u32[]{:S(2)}) copy-start(f32[256]{0:T(256)} %param.24) | copy-start | bytes 3076
  77.7 7.5 %copy-start.8 = (s32[8]{0:T(128)S(1)}, s32[8]{0:T(128)}, u32[]{:S(2)}) copy-start(s32[8]{0:T(128)} %counts_ref.1) | copy-start | bytes 100

commit v2 on v1

--- a/solution.py
+++ b/solution.py
@@ -72,13 +72,11 @@
     return cotan * (cdf + pre * jnp.exp(-0.5 * pre * pre) * (1.0 / math.sqrt(2.0 * math.pi)))
 
 
-def rank_slots(dest, target, code_ref, send_ref):
-    hit = lax.broadcasted_iota(jnp.int32, (256, 1024), 0) == dest
-    one_hot = jnp.where(hit, 1.0, 0.0).astype(BF16)
+def earlier_same(one_hot, hit):
     lane = lanes_of((128, 256))
     earlier = (lax.broadcasted_iota(jnp.int32, (128, 256), 0) < lane) | (lane >= 128)
     earlier = jnp.where(earlier, 1.0, 0.0).astype(BF16)
-    before = jnp.zeros((256, 128), F32)
+    before = jnp.zeros((hit.shape[0], 128), F32)
     ranks = []
     for block in range(8):
         at = slice(block * 128, block * 128 + 128)
@@ -86,7 +84,13 @@
         own = jnp.where(hit[:, at], count[:, :128] + before, 0.0)
         ranks.append(jnp.sum(own, axis=0, keepdims=True))
         before = before + count[:, 128:]
-    rank = jnp.concatenate(ranks, axis=1).astype(jnp.int32)
+    return jnp.concatenate(ranks, axis=1).astype(jnp.int32), before
+
+
+def rank_slots(dest, target, code_ref, send_ref):
+    hit = lax.broadcasted_iota(jnp.int32, (256, 1024), 0) == dest
+    one_hot = jnp.where(hit, 1.0, 0.0).astype(BF16)
+    rank, _ = earlier_same(one_hot, hit)
     code_ref[...] = dest * 8 + rank
     number = target + 1
     group = lax.broadcasted_iota(jnp.int32, (16, 1024), 0) == (dest >> 5)
@@ -122,17 +126,17 @@
     for copy in small:
         copy.start()
     loads = []
-    for step in range(8):
-        at = pl.ds(step * 8, 8)
+    for step in range(2):
+        at = pl.ds(step * 32, 32)
         loads.append(pltpu.make_async_copy(pre_hbm.at[at], pre_ref.at[at], sems.at[step, 0]))
         loads.append(pltpu.make_async_copy(cotan_hbm.at[at], cotan_ref.at[at], sems.at[step, 1]))
     for copy in loads:
         copy.start()
     for copy in small:
         copy.wait()
-    rank_slots(dest_ref[...], target_ref[...], code_ref, send_ref)
     for copy in loads:
         copy.wait()
+    rank_slots(dest_ref[...], target_ref[...], code_ref, send_ref)
     for step in range(8):
         at = pl.ds(step * 8, 8)
         pre = pre_ref[at].astype(F32).reshape(512, 128)
@@ -179,21 +183,26 @@
         halves = []
         for part in range(2):
             at = slice(part * 16, part * 16 + 16)
-            high, low = split(jnp.concatenate([hat[at], other[at]], axis=0))
+            modes = jnp.concatenate([hat[at], other[at]], axis=0)
+            second = (lax.broadcasted_iota(jnp.int32, (32, 128), 0) & 1) == 1
+            modes = jnp.concatenate(
+                [jnp.where(second, 0.0, modes), jnp.where(second, modes, 0.0)], axis=1
+            )
+            high, low = split(modes)
             first = (kx * 32 + part * 16) * 64
-            cross = dot(
-                jnp.concatenate([high, low], axis=0), spectral_ref[first : first + 1024, :], NT
-            )
+            weights = spectral_ref[first : first + 1024, :].reshape(8, 2, 64, 128)
+            weights = jnp.concatenate([weights[:, 0], weights[:, 1]], axis=2).reshape(512, 256)
+            cross = dot(jnp.concatenate([high, low], axis=0), weights, NT)
             cross = cross[:32] + cross[32:]
             row = lax.broadcasted_iota(jnp.int32, (16, 128), 0)
             real = jnp.zeros((16, 128), F32)
             imag = jnp.zeros((16, 128), F32)
-            for pair in range(8):
-                own = (row >> 1) == pair
+            for pair in range(4):
+                own = (row >> 2) == pair
                 at = slice(pair * 128, pair * 128 + 128)
                 real = jnp.where(own, cross[:16, at], real)
                 imag = jnp.where(own, cross[16:, at], imag)
-            even = (row & 1) == 0
+            even = (row & 2) == 0
             left = lanes_of((16, 128)) < 64
             halves.append(
                 jnp.where(
@@ -253,8 +262,38 @@
             )
 
 
-def local_kernel(pre_ref, cotan_ref, weight_ref, voxel_ref, after_hbm, out_ref, table_ref):
+ROOM = 1280
+
+
+def order_kernel(code_ref, voxel_ref, after_hbm, place_ref, entry_ref, count_ref):
     del after_hbm
+    code, voxel = code_ref[...], voxel_ref[...]
+    kind = ((voxel >> 7) & 1) * 2 + (code & 1)
+    hit = lax.broadcasted_iota(jnp.int32, (16, 1024), 0) == kind
+    number, total = earlier_same(jnp.where(hit, 1.0, 0.0).astype(BF16), hit)
+    place_ref[...] = kind * ROOM + number
+    entry_ref[...] = ((voxel >> 8) * 128 + (voxel & 127)) * 2048 + (code >> 1)
+    own = lax.broadcasted_iota(jnp.int32, (16, 128), 0) == lanes_of((16, 128))
+    count_ref[...] = jnp.sum(jnp.where(own, total, 0.0), axis=0, keepdims=True).astype(jnp.int32)
+
+
+def local_kernel(
+    pre_ref,
+    cotan_ref,
+    weight_ref,
+    kernel_ref,
+    code_ref,
+    voxel_ref,
+    place_ref,
+    entry_ref,
+    count_ref,
+    scale_ref,
+    shift_ref,
+    list_ref,
+    table_ref,
+):
+    scale_ref[...] = jnp.zeros_like(scale_ref)
+    shift_ref[...] = jnp.zeros_like(shift_ref)
 
     def fill(step, carry):
         at = pl.ds(step * 4, 4)
@@ -269,49 +308,67 @@
         return carry
 
     lax.fori_loop(0, 16, fill, 0)
-
-    def take(step, carry):
+    side = lanes_of((1, 128)) >> 6
+
+    def place(step, carry):
         for part in range(16):
             slot = step * 16 + part
-            out_ref[pl.ds(slot, 1), :] = table_ref[pl.ds(voxel_ref[slot], 1), :]
+            code = code_ref[slot]
+            voxel = voxel_ref[slot]
+            scale = kernel_ref[pl.ds(slot, 1), :]
+            shift = table_ref[pl.ds(voxel, 1), :] * scale
+            mask = side == (code & 1)
+            at = pl.ds(code >> 1, 1)
+            pltpu.store(scale_ref.at[at, :], scale, mask=mask)
+            pltpu.store(shift_ref.at[at, :], shift, mask=mask)
+            list_ref[place_ref[slot]] = entry_ref[slot]
         return carry
 
-    lax.fori_loop(0, 64, take, 0)
+    lax.fori_loop(0, 64, place, 0)
+    for kind in range(4):
+        for part in range(16):
+            list_ref[kind * ROOM + count_ref[kind] + part] = 1024
+        list_ref[kind * ROOM + ROOM - 1] = count_ref[kind]
 
 
 def slots_kernel(
     in_ref,
     table_ref,
-    kernel_hbm,
-    local_hbm,
-    code_ref,
-    voxel_ref,
+    scale_hbm,
+    shift_hbm,
+    list_hbm,
     out_ref,
     numbers_ref,
     field_ref,
-    kernel_ref,
-    local_ref,
+    same_ref,
+    other_ref,
+    scale_ref,
+    shift_ref,
+    list_ref,
     sems,
 ):
+    list_copy = pltpu.make_async_copy(list_hbm, list_ref, sems.at[2])
+    list_copy.start()
     copies = (
-        pltpu.make_async_copy(kernel_hbm, kernel_ref, sems.at[0]),
-        pltpu.make_async_copy(local_hbm, local_ref, sems.at[1]),
+        pltpu.make_async_copy(scale_hbm, scale_ref, sems.at[0]),
+        pltpu.make_async_copy(shift_hbm, shift_ref, sems.at[1]),
     )
     for copy in copies:
         copy.start()
-    out_ref[...] = jnp.zeros_like(out_ref)
     numbers_ref[...] = in_ref[pl.ds(64, 32, stride=65), :]
+    same_ref[...] = jnp.zeros_like(same_ref)
+    other_ref[...] = jnp.zeros_like(other_ref)
 
     def fill(step, carry):
         for part in range(4):
             stacks = []
             first = step * 8 + part * 2
             for h in range(2):
-                data = in_ref[pl.ds(first + h, 32, stride=65), :]
-                other = swap(data)
-                left = lanes_of(data.shape) < 64
-                real_high, real_low = split(jnp.where(left, data, other))
-                imag_high, imag_low = split(-jnp.where(left, other, data))
+                even = in_ref[pl.ds(2 * (first + h), 32, stride=65), :]
+                odd = in_ref[pl.ds(2 * (first + h) + 1, 32, stride=65), :]
+                left = lanes_of(even.shape) < 64
+                real_high, real_low = split(jnp.where(left, even, swap(odd)))
+                imag_high, imag_low = split(-jnp.where(left, swap(even), odd))
                 stacks.append(
                     jnp.concatenate(
                         [real_high, real_low, real_high, imag_high, imag_low, imag_high], axis=0
@@ -323,40 +380,52 @@
                 field_ref[pl.ds(at, 128), :] = field[:, h * 128 : h * 128 + 128]
         return carry
 
-    lax.fori_loop(0, 8, fill, 0, unroll=2)
+    lax.fori_loop(0, 4, fill, 0, unroll=2)
     side = lanes_of((1, 128)) >> 6
+    list_copy.wait()
+    for kind in range(4):
+        into_ref = same_ref if kind in (0, 3) else other_ref
+        mask = side == (kind >> 1)
+
+        def take(step, carry, kind=kind, into_ref=into_ref, mask=mask):
+            entries = [list_ref[kind * ROOM + step * 16 + part] for part in range(16)]
+            rows = [field_ref[pl.ds(entry >> 11, 1), :] for entry in entries]
+            for entry, row in zip(entries, rows):
+                pltpu.store(into_ref.at[pl.ds(entry & 2047, 1), :], row, mask=mask)
+            return carry
+
+        lax.fori_loop(0, (list_ref[kind * ROOM + ROOM - 1] + 15) >> 4, take, 0)
     for copy in copies:
         copy.wait()
-
-    def place(step, carry):
-        for part in range(16):
-            slot = step * 16 + part
-            code = code_ref[slot]
-            value = (
-                field_ref[pl.ds(voxel_ref[slot], 1), :] + local_ref[pl.ds(slot, 1), :]
-            ) * kernel_ref[pl.ds(slot, 1), :]
-            pltpu.store(out_ref.at[pl.ds(code >> 1, 1), :], value, mask=side == (code & 1))
-        return carry
-
-    lax.fori_loop(0, 64, place, 0, unroll=2)
-
-
-def gather_kernel(in_ref, numbers_ref, out_ref):
+    for block in range(8):
+        at = slice(block * 128, block * 128 + 128)
+        out_ref[at] = (same_ref[at] + swap(other_ref[at])) * scale_ref[at] + shift_ref[at]
+
+
+def gather_kernel(in_ref, numbers_ref, out_hbm, out_ref, sems):
     numbers = numbers_ref[...] - 1.0
-    point = lanes_of((256, 1024)).astype(F32)
-    total = jnp.zeros((128, 1024), F32)
+    sides = []
     for pair in range(4):
-        data = in_ref[pl.ds(pair, 256, stride=4), :].T
-        high, low = split(data)
+        high, low = split(in_ref[pl.ds(pair, 256, stride=4), :].T)
         for h in range(2):
             at = slice(h * 64, h * 64 + 64)
             rank = pair * 2 + h
             column = jnp.concatenate(
                 [numbers[:, g * 8 + rank : g * 8 + rank + 1] for g in range(8)], axis=0
             )
-            one_hot = jnp.where(column == point, 1.0, 0.0).astype(BF16)
-            total = total + dot(jnp.concatenate([high[at], low[at]], axis=0), one_hot)
-    out_ref[...] = total[:64] + total[64:]
+            sides.append((jnp.concatenate([high[at], low[at]], axis=0), column))
+    copies = []
+    for half in range(2):
+        point = lanes_of((256, 512)).astype(F32) + half * 512.0
+        total = jnp.zeros((128, 512), F32)
+        for data, column in sides:
+            total = total + dot(data, jnp.where(column == point, 1.0, 0.0).astype(BF16))
+        at = pl.ds(half * 512, 512)
+        out_ref[:, half * 512 : half * 512 + 512] = total[:64] + total[64:]
+        copies.append(pltpu.make_async_copy(out_ref.at[:, at], out_hbm.at[:, at], sems.at[half]))
+        copies[-1].start()
+    for copy in copies:
+        copy.wait()
 
 
 VMEM = pl.BlockSpec(memory_space=pltpu.VMEM)
@@ -420,7 +489,7 @@
             pltpu.VMEM((128, 256), BF16),
             pltpu.VMEM((1, 1024), jnp.int32),
             pltpu.VMEM((1, 1024), jnp.int32),
-            pltpu.SemaphoreType.DMA((8, 2)),
+            pltpu.SemaphoreType.DMA((2, 2)),
             pltpu.SemaphoreType.DMA((3,)),
         ],
     )(
@@ -444,7 +513,7 @@
     net_in = jnp.concatenate([kernel_inputs, jnp.ones((1, 1024), F32), jnp.zeros((1, 1024), F32)])
     first_layer = jnp.concatenate([w_in, b_in[None], jnp.zeros((1, 512), F32)])
     kernel = call(
-        kernel_net_kernel, pltpu.HBM((1024, 128), F32), [VMEM] * 6 + [SMEM, ANY]
+        kernel_net_kernel, shape((1024, 128), F32), [VMEM] * 6 + [SMEM, ANY]
     )(
         net_in,
         first_layer,
@@ -457,27 +526,57 @@
     )
     weight = jnp.concatenate([pointwise, pointwise], axis=0)
     weight = jnp.concatenate([weight, weight], axis=1)
-    own = call(
+    place, entry, count = call(
+        order_kernel,
+        (
+            shape((1, 1024), jnp.int32),
+            shape((1, 1024), jnp.int32),
+            shape((1, 128), jnp.int32),
+        ),
+        [VMEM, VMEM, ANY],
+    )(code.reshape(1, 1024), voxel_index.reshape(1, 1024), columns)
+    count = count.reshape(128)
+    scale, shift, entries = call(
         local_kernel,
-        pltpu.HBM((1024, 128), F32),
-        [VMEM, VMEM, VMEM, SMEM, ANY],
+        (pltpu.HBM((1024, 128), F32), pltpu.HBM((1024, 128), F32), shape((4 * ROOM,), jnp.int32)),
+        [VMEM, VMEM, VMEM, VMEM, SMEM, SMEM, SMEM, SMEM, SMEM],
         [pltpu.VMEM((8192, 128), F32)],
-    )(pre, cotan, weight, voxel_index, columns)
+        out_specs=(VMEM, VMEM, SMEM),
+    )(
+        pre,
+        cotan,
+        weight,
+        kernel,
+        code,
+        voxel_index,
+        place.reshape(1024),
+        entry.reshape(1024),
+        count,
+    )
 
     columns = exchange(columns, "slab", 32)
     slots, numbers = call(
         slots_kernel,
         (shape((1024, 128), F32), shape((32, 128), F32)),
-        [VMEM, VMEM, HBM, HBM, SMEM, SMEM],
+        [VMEM, VMEM, HBM, HBM, HBM],
         [
-            pltpu.VMEM((8192, 128), F32),
+            pltpu.VMEM((4096, 128), F32),
+            pltpu.VMEM((1032, 128), F32),
+            pltpu.VMEM((1032, 128), F32),
             pltpu.VMEM((1024, 128), F32),
             pltpu.VMEM((1024, 128), F32),
-            pltpu.SemaphoreType.DMA((2,)),
+            pltpu.SMEM((4 * ROOM,), jnp.int32),
+            pltpu.SemaphoreType.DMA((3,)),
         ],
-    )(columns, inverse, in_hbm(kernel), in_hbm(own), code, voxel_index)
+    )(columns, inverse, in_hbm(scale), in_hbm(shift), in_hbm(entries))
     slots = exchange(slots, ("grp", "slab"), 256)
-    return call(gather_kernel, shape((64, 1024), F32), [VMEM, VMEM])(slots, numbers)
+    return call(
+        gather_kernel,
+        shape((64, 1024), F32),
+        [VMEM, VMEM],
+        [pltpu.VMEM((64, 1024), F32), pltpu.SemaphoreType.DMA((2,))],
+        out_specs=HBM,
+    )(slots, numbers)
 
 
 def solution(mesh):

time: 141 us -> 139 us (0.986)
  waiting for transfers between devices: 12.1 us -> 8.96 us
    all_to_all x1, waiting for transfers between devices: 12.1 us -> 8.96 us  [exchange(): lax.all_to_all(rows.reshape(chunks), axis, split_axis=0, concat_axis=0, t...]
    pallas_call x3 -> x4, Pallas kernels: 14.6 us -> 16.8 us  [the longest x1 10.3 us: local(): call(local_kernel, (pltpu.HBM((1024, 128), F32), pltpu.HBM((1024, 128), F...]
  transfers between devices with their start and end apart: 1 -> 1, of which waited for: 1 -> 1; matrix products, arithmetic and copies ran while one was open for 0% -> 0% of each run, Pallas kernels for 9% -> 11%
where the time goes in v2:
time: 139 us; the launch traced here: 138 us
  blocking collectives  94.3 us (68%)
  Pallas kernels  28.5 us (21%)
  waiting for transfers between devices  8.96 us (6%)
  starting transfers between devices  4.94 us (4%)
    all_to_all x4, blocking collectives, exchange(): lax.all_to_all(rows.reshape(chunks), axis, split_axis=0, concat_axis=0, t...  94.3 us
    pallas_call x1, Pallas kernels, local(): call(local_kernel, (pltpu.HBM((1024, 128), F32), pltpu.HBM((1024, 128), F...  10.3 us
    all_to_all x1, waiting for transfers between devices, exchange(): lax.all_to_all(rows.reshape(chunks), axis, split_axis=0, concat_axis=0, t...  8.96 us
    all_to_all x1, starting transfers between devices, exchange(): lax.all_to_all(rows.reshape(chunks), axis, split_axis=0, concat_axis=0, t...  4.94 us
    pallas_call x1, Pallas kernels, local(): call(kernel_net_kernel, shape((1024, 128), F32), [VMEM] * 6 + [SMEM, ANY])  4.53 us
    pallas_call x1, Pallas kernels, local(): call(modes_z_kernel, (shape((2048, 128), F32), shape((1, 1024), jnp.int32...  4.18 us
    pallas_call x1, Pallas kernels, local(): call(slots_kernel, (shape((1024, 128), F32), shape((32, 128), F32)), [VME...  3.22 us
  transfers between devices with their start and end apart: 1, of which 1 were waited for; matrix products, arithmetic and copies ran while one was open for 0% of the time, Pallas kernels for 11%

profile of v2, /device:TPU:1, one launch (start us, length us, event | category | flops | bytes accessed | tf_op | source)
XLA Modules:
  0.0 138.3 jit_solution(12914279014348394646)
XLA Ops:
  0.0 4.2 %shard_map.163 = (f32[2048,128]{1,0:T(8,128)S(1)}, s32[1,1024]{1,0:T(1,128)S(1)}, f32[8,256]{1,0:T(8,128)S(1)}) custom-call(bf16[64,64,128]{2,1,0:T(8,128)(2,1)} %bitcast.29, bf16[64,64,128]{2,1,0:T(8,128)(2,1)} %bitcast.31, bf16[128,256]{1,0:T(8,128)(2,1)} %constant.3.clone.table_hbm.table_ref.forward_ref, s32[1,1024]{1,0:T(1,128)} %bitcast.49, ...), custom_call_target="tpu_custom_call" | custom-call | tf_op jit(solution)/shard_map/pallas_call | solution.py:482
  4.2 0.0 copy-start.4
  4.2 36.6 %all_to_all.25 = f32[32,64,128]{2,1,0:T(8,128)S(1)} all-to-all(f32[32,64,128]{2,1,0:T(8,128)S(1)} %bitcast.38), channel_id=1, replica_groups=mesh['grp'=8,'slab'=32] {'slab'}, dimensions={0} | all-to-all | bytes 2097152 | tf_op jit(solution)/shard_map/all_to_all | solution.py:456
  40.8 0.6 shard_map.164
  41.4 15.6 %all_to_all.26 = f32[8,64,128]{2,1,0:T(8,128)S(1)} all-to-all(f32[8,64,128]{2,1,0:T(8,128)S(1)} %bitcast.39), channel_id=1, replica_groups=mesh['grp'=8,'slab'=32] {'grp'}, dimensions={0} | all-to-all | bytes 524288 | tf_op jit(solution)/shard_map/all_to_all | solution.py:456
  57.0 2.0 %shard_map.165 = f32[528,128]{1,0:T(8,128)S(1)} custom-call(f32[512,128]{1,0:T(8,128)S(1)} %bitcast.40, bf16[8192,128]{1,0:T(8,128)(2,1)S(1)} %bitcast.34, bf16[128,256]{1,0:T(8,128)(2,1)S(1)} %copy-done.4, bf16[128,192]{1,0:T(8,128)(2,1)S(1)} %copy-done.3, f32[8,256]{1,0:T(8,128)S(1)} %get-tuple-element.17.targets_ref), custom_call_target="tpu_custom_call" | custom-call | tf_op jit(solution)/shard_map/pallas_call | solution.py:507
  59.1 10.6 %all_to_all.27 = f32[8,1,8448]{2,1,0:T(1,128)S(1)} all-to-all(f32[8,1,8448]{2,1,0:T(1,128)S(1)} %bitcast.37), channel_id=1, replica_groups=mesh['grp'=8,'slab'=32] {'grp'}, dimensions={0} | all-to-all | bytes 540672 | tf_op jit(solution)/shard_map/all_to_all | solution.py:456
  69.7 1.6 %shard_map.166.after_hbm = f32[2080,128]{1,0:T(8,128)} custom-call(f32[528,128]{1,0:T(8,128)S(1)} %bitcast.36, bf16[128,192]{1,0:T(8,128)(2,1)S(1)} %copy-done.3), custom_call_target="tpu_custom_call" | custom-call | tf_op jit(solution)/shard_map/pallas_call | solution.py:511
  71.3 4.9 %all-to-all-start.3 = ((f32[32,1,8320]{2,1,0:T(1,128)}), f32[32,1,8320]{2,1,0:T(1,128)S(1)}, u32[]{:S(2)}, u32[]{:S(2)}) async-start(f32[32,1,8320]{2,1,0:T(1,128)} %bitcast.11), calls=%async_computation.3 | async-start | bytes 2129920 | tf_op jit(solution)/shard_map/all_to_all | solution.py:456
  76.3 0.1 pad.9.clone
  76.4 0.1 pad.8.clone
  76.5 0.1 maximum_bitcast_fusion.b_out_ref
  76.5 0.1 maximum_maximum_fusion.weight_ref
  76.7 0.1 maximum_maximum_fusion.2.w_in_ref
  76.8 0.1 maximum_maximum_fusion.1.in_ref
  76.8 0.2 shard_map.168
  77.0 0.3 copy-done.5
  77.3 4.5 %shard_map.167.kernel_ref = f32[1024,128]{1,0:T(8,128)S(1)} custom-call(f32[8,1024]{1,0:T(8,128)S(1)} %maximum_maximum_fusion.1.in_ref, f32[8,512]{1,0:T(8,128)S(1)} %maximum_maximum_fusion.2.w_in_ref, f32[512,256]{1,0:T(8,128)S(1)} %copy-done.5, f32[1,256]{1,0:T(1,128)S(1)} %bitcast.46, f32[128,256]{1,0:T(8,128)S(1)} %pad_maximum_fusion.w_out_ref, ...), custom_call_target="tpu_custom_call" | custom-call | tf_op jit(solution)/shard_map/pallas_call | solution.py:515
  81.9 10.3 %shard_map.169 = (f32[1024,128]{1,0:T(8,128)}, f32[1024,128]{1,0:T(8,128)}, s32[5120]{0:T(1024)S(1)}) custom-call(bf16[64,64,128]{2,1,0:T(8,128)(2,1)S(1)} %bitcast.30, bf16[64,64,128]{2,1,0:T(8,128)(2,1)S(1)} %bitcast.32, bf16[128,128]{1,0:T(8,128)(2,1)S(1)} %maximum_maximum_fusion.weight_ref, f32[1024,128]{1,0:T(8,128)S(1)} %shard_map.167.kernel_ref, ...), custom_call_target="tpu_custom_call" | custom-call | tf_op jit(solution)/shard_map/pallas_call | solution.py:539
  92.2 0.6 copy-done.6
  92.8 9.0 %all-to-all-done.3 = f32[32,1,8320]{2,1,0:T(1,128)S(1)} async-done(((f32[32,1,8320]{2,1,0:T(1,128)}), f32[32,1,8320]{2,1,0:T(1,128)S(1)}, u32[]{:S(2)}, u32[]{:S(2)}) %all-to-all-start.3) | async-done | bytes 1064992 | tf_op jit(solution)/shard_map/all_to_all | solution.py:456
  101.8 3.2 %shard_map.170 = (f32[1024,128]{1,0:T(8,128)S(1)}, f32[32,128]{1,0:T(8,128)S(1)}) custom-call(f32[2080,128]{1,0:T(8,128)S(1)} %bitcast.28, bf16[128,192]{1,0:T(8,128)(2,1)S(1)} %copy-done.3, f32[1024,128]{1,0:T(8,128)} %get-tuple-element.22.scale_hbm, f32[1024,128]{1,0:T(8,128)} %get-tuple-element.23.shift_hbm, s32[5120]{0:T(1024)} %copy-done.6), custom_call_target="tpu_custom_call" | custom-call | tf_op jit(solution)/shard_map/pallas_call | solution.py:558
  105.0 31.5 %all_to_all.28 = f32[256,1,512]{2,1,0:T(1,128)S(1)} all-to-all(f32[256,1,512]{2,1,0:T(1,128)S(1)} %bitcast.41), channel_id=1, replica_groups=mesh['grp'=8,'slab'=32] {'grp','slab'}, dimensions={0} | all-to-all | bytes 1048576 | tf_op jit(solution)/shard_map/all_to_all | solution.py:456
  136.5 1.8 %shard_map.171 = f32[64,1024]{1,0:T(8,128)} custom-call(f32[1024,128]{1,0:T(8,128)S(1)} %bitcast.35, f32[32,128]{1,0:T(8,128)S(1)} %get-tuple-element.26.numbers_ref), custom_call_target="tpu_custom_call" | custom-call | tf_op jit(solution)/shard_map/pallas_call | solution.py:573
  (30 shorter events, 0.1 us)
Async XLA Ops:
  4.2 36.6 %copy-start.4 = (bf16[128,256]{1,0:T(8,128)(2,1)S(1)}, bf16[128,256]{1,0:T(8,128)(2,1)}, u32[]{:S(2)}) copy-start(bf16[128,256]{1,0:T(8,128)(2,1)} %constant.3.clone.table_hbm.table_ref.forward_ref) | copy-start | bytes 196612
  4.2 52.8 %copy-start.2 = (bf16[1,4,32,64,128]{4,3,2,1,0:T(8,128)(2,1)S(1)}, bf16[1,4,32,64,128]{4,3,2,1,0:T(8,128)(2,1)}, u32[]{:S(2)}) copy-start(bf16[1,4,32,64,128]{4,3,2,1,0:T(8,128)(2,1)} %param.20) | copy-start | bytes 6291460
  40.8 16.2 %copy-start.3 = (bf16[128,192]{1,0:T(8,128)(2,1)S(1)}, bf16[128,192]{1,0:T(8,128)(2,1)}, u32[]{:S(2)}) copy-start(bf16[128,192]{1,0:T(8,128)(2,1)} %constant.10.clone.inverse_ref.table_ref) | copy-start | bytes 147460
  71.3 5.2 %copy-start.15 = (f32[64]{0:T(128)S(1)}, f32[64]{0:T(128)}, u32[]{:S(2)}) copy-start(f32[64]{0:T(128)} %param.26) | copy-start | bytes 772
  71.3 5.3 %copy-start.12 = (bf16[64,64]{1,0:T(8,128)(2,1)S(1)}, bf16[64,64]{1,0:T(8,128)(2,1)}, u32[]{:S(2)}) copy-start(bf16[64,64]{1,0:T(8,128)(2,1)} %param.19) | copy-start | bytes 24580
  71.3 5.3 %copy-start.10 = (f32[256,64]{0,1:T(8,128)S(1)}, f32[256,64]{0,1:T(8,128)}, u32[]{:S(2)}) copy-start(f32[256,64]{0,1:T(8,128)} %param.25) | copy-start | bytes 196612
  71.3 5.4 %copy-start.13 = (f32[6,512]{1,0:T(8,128)S(1)}, f32[6,512]{1,0:T(8,128)}, u32[]{:S(2)}) copy-start(f32[6,512]{1,0:T(8,128)} %param.21) | copy-start | bytes 36868
  71.3 5.4 %copy-start.14 = (f32[512]{0:T(512)S(1)}, f32[512]{0:T(512)}, u32[]{:S(2)}) copy-start(f32[512]{0:T(512)} %param.22) | copy-start | bytes 6148
  71.3 5.5 %copy-start.11 = (f32[6,1024]{1,0:T(8,128)S(1)}, f32[6,1024]{1,0:T(8,128)}, u32[]{:S(2)}) copy-start(f32[6,1024]{1,0:T(8,128)} %param.27) | copy-start | bytes 73732
  71.3 5.5 %copy-start.7 = (s32[1024]{0:T(1024)S(1)}, s32[1024]{0:T(1024)}, u32[]{:S(2)}) copy-start(s32[1024]{0:T(1024)} %voxel_ref.1) | copy-start | bytes 12292
  71.3 30.5 %all-to-all-start.3 = ((f32[32,1,8320]{2,1,0:T(1,128)}), f32[32,1,8320]{2,1,0:T(1,128)S(1)}, u32[]{:S(2)}, u32[]{:S(2)}) async-start(f32[32,1,8320]{2,1,0:T(1,128)} %bitcast.11), calls=%async_computation.3 | async-start | bytes 2129920 | tf_op jit(solution)/shard_map/all_to_all | solution.py:456
  76.3 1.0 copy-start.5
  76.3 1.0 copy-start.8
  76.3 1.0 copy-start.9
  77.3 4.5 %copy-start = (bf16[4,16,64,128]{3,2,1,0:T(8,128)(2,1)S(1)}, bf16[4,16,64,128]{3,2,1,0:T(8,128)(2,1)}, u32[]{:S(2)}) copy-start(bf16[4,16,64,128]{3,2,1,0:T(8,128)(2,1)} %param.17) | copy-start | bytes 3145732
  77.3 4.6 %copy-start.1 = (bf16[4,16,64,128]{3,2,1,0:T(8,128)(2,1)S(1)}, bf16[4,16,64,128]{3,2,1,0:T(8,128)(2,1)}, u32[]{:S(2)}) copy-start(bf16[4,16,64,128]{3,2,1,0:T(8,128)(2,1)} %param.18) | copy-start | bytes 3145732
  92.2 0.6 copy-start.6

commit v3 on v2

--- a/solution.py
+++ b/solution.py
@@ -14,6 +14,8 @@
 NG = 128
 MODES = 32
 CH = 64
+OUT_STEP, OUT_FIRST = 31, 15
+BACK_STEP, BACK_FIRST = 31, 15
 NN = (((1,), (0,)), ((), ()))
 NT = (((1,), (1,)), ((), ()))
 TN = (((0,), (0,)), ((), ()))
@@ -23,20 +25,36 @@
     return lax.dot_general(a, b, dims, precision=precision, preferred_element_type=F32)
 
 
-def tables():
-    position = np.arange(NG)
-    frequency = np.arange(MODES) - MODES // 2
-    angle = (np.outer(frequency, position) % NG) * (2.0 * math.pi / NG)
+def back_slab(chunk):
+    return (chunk * BACK_STEP + BACK_FIRST) & 31
+
+
+OUT_SLABS = [(chunk * OUT_STEP + OUT_FIRST) & 31 for chunk in range(32)]
+BACK_SLABS = [back_slab(chunk) for chunk in range(32)]
+OUT_X = [slab * 4 + part for slab in OUT_SLABS for part in range(4)]
+BACK_X = [slab * 4 + part for slab in BACK_SLABS for part in range(4)]
+
+
+def waves(modes, positions):
+    frequency = np.array(modes) - MODES // 2
+    angle = (np.outer(frequency, np.array(positions)) % NG) * (2.0 * math.pi / NG)
     parts = []
     for table in (np.cos(angle), np.sin(angle)):
         high = table.astype(np.float32).astype(BF16)
         low = (table - high.astype(np.float64)).astype(np.float32).astype(BF16)
         parts.append((high, low))
-    (ch, cl), (sh, sl) = parts
+    return parts
+
+
+def forward_table(modes, positions):
+    (ch, cl), (sh, sl) = waves(modes, positions)
     zero = np.zeros_like(ch)
-    forward = np.block([[ch, ch], [sh, sh], [cl, zero], [sl, zero]])
-    inverse = np.concatenate([ch.T, ch.T, cl.T, sh.T, sh.T, sl.T], axis=1)
-    return forward, inverse
+    return jnp.asarray(np.block([[ch, ch], [sh, sh], [cl, zero], [sl, zero]]))
+
+
+def inverse_table(modes, positions):
+    (ch, cl), (sh, sl) = waves(modes, positions)
+    return jnp.asarray(np.concatenate([ch.T, ch.T, cl.T, sh.T, sh.T, sl.T], axis=1))
 
 
 def split(x):
@@ -171,20 +189,29 @@
 def mix_kernel(in_ref, spectral_ref, forward_ref, inverse_ref, targets_ref, out_ref):
     for half in range(2):
         out_ref[pl.ds(64 + half, 8, stride=66), :] = targets_ref[:, half * 128 : half * 128 + 128]
+    data = jnp.concatenate(
+        [
+            jnp.concatenate(
+                [in_ref[g * 64 + kx * 16 : g * 64 + kx * 16 + 16, :] for g in range(8)], axis=0
+            )
+            for kx in range(4)
+        ],
+        axis=1,
+    )
+    high, low = split(data)
+    product = dot(forward_ref[...], jnp.concatenate([high, low], axis=0))
+    row = lax.broadcasted_iota(jnp.int32, (16, 128), 0)
+    left = lanes_of((16, 128)) < 64
+    even = (row & 2) == 0
+    second = (lax.broadcasted_iota(jnp.int32, (32, 128), 0) & 1) == 1
+    crosses = []
     for kx in range(4):
-        data = jnp.concatenate(
-            [in_ref[g * 64 + kx * 16 : g * 64 + kx * 16 + 16, :] for g in range(8)], axis=0
-        )
-        high, low = split(data)
-        product = dot(forward_ref[...], jnp.concatenate([high, low], axis=0))
-        cos_part, sin_part = forward_parts(product, 0, 128)
+        cos_part, sin_part = forward_parts(product, kx * 128, 128)
         hat = cos_part + turn(sin_part)
         other = turn(hat)
-        halves = []
         for part in range(2):
             at = slice(part * 16, part * 16 + 16)
             modes = jnp.concatenate([hat[at], other[at]], axis=0)
-            second = (lax.broadcasted_iota(jnp.int32, (32, 128), 0) & 1) == 1
             modes = jnp.concatenate(
                 [jnp.where(second, 0.0, modes), jnp.where(second, modes, 0.0)], axis=1
             )
@@ -192,18 +219,20 @@
             first = (kx * 32 + part * 16) * 64
             weights = spectral_ref[first : first + 1024, :].reshape(8, 2, 64, 128)
             weights = jnp.concatenate([weights[:, 0], weights[:, 1]], axis=2).reshape(512, 256)
-            cross = dot(jnp.concatenate([high, low], axis=0), weights, NT)
+            crosses.append(dot(jnp.concatenate([high, low], axis=0), weights, NT))
+    stacks = []
+    for kx in range(4):
+        halves = []
+        for part in range(2):
+            cross = crosses[kx * 2 + part]
             cross = cross[:32] + cross[32:]
-            row = lax.broadcasted_iota(jnp.int32, (16, 128), 0)
-            real = jnp.zeros((16, 128), F32)
-            imag = jnp.zeros((16, 128), F32)
-            for pair in range(4):
+            real = cross[:16, 0:128]
+            imag = cross[16:, 0:128]
+            for pair in range(1, 4):
                 own = (row >> 2) == pair
                 at = slice(pair * 128, pair * 128 + 128)
                 real = jnp.where(own, cross[:16, at], real)
                 imag = jnp.where(own, cross[16:, at], imag)
-            even = (row & 2) == 0
-            left = lanes_of((16, 128)) < 64
             halves.append(
                 jnp.where(
                     left,
@@ -211,17 +240,21 @@
                     jnp.where(even, swap(imag), imag),
                 )
             )
-        mixed = jnp.concatenate(halves, axis=0) * (1.0 / float(NG) ** 3)
-        field = dot(inverse_ref[...], inverse_stack(mixed))
+        stacks.append(inverse_stack(jnp.concatenate(halves, axis=0) * (1.0 / float(NG) ** 3)))
+    field = dot(inverse_ref[...], jnp.concatenate(stacks, axis=1))
+    for kx in range(4):
         for g in range(8):
-            out_ref[g * 66 + kx * 16 : g * 66 + kx * 16 + 16, :] = field[g * 16 : g * 16 + 16]
+            out_ref[g * 66 + kx * 16 : g * 66 + kx * 16 + 16, :] = field[
+                g * 16 : g * 16 + 16, kx * 128 : kx * 128 + 128
+            ]
 
 
 def field_x_kernel(in_ref, table_ref, out_ref):
     number = jnp.concatenate(
         [in_ref[pl.ds(64 + half, 8, stride=66), :] for half in range(2)], axis=1
     ).astype(jnp.int32)
-    own = (lanes_of((32, 256)) >> 3) == lax.broadcasted_iota(jnp.int32, (32, 256), 0)
+    slab = back_slab(lax.broadcasted_iota(jnp.int32, (32, 256), 0))
+    own = (lanes_of((32, 256)) >> 3) == slab
     total = jnp.zeros((64, 128), F32)
     for g in range(8):
         row = number[g : g + 1]
@@ -234,8 +267,7 @@
     for y in range(0, 16, 2):
         stacks = []
         for h in range(2):
-            low = in_ref[pl.ds(y + h, 4, stride=16), :]
-            parts = [low] + [in_ref[pl.ds(g * 66 + y + h, 4, stride=16), :] for g in range(1, 8)]
+            parts = [in_ref[pl.ds(g * 66 + y + h, 4, stride=16), :] for g in range(8)]
             stacks.append(inverse_stack(jnp.concatenate(parts, axis=0)))
         field = dot(table_ref[...], jnp.concatenate(stacks, axis=1))
         for h in range(2):
@@ -355,7 +387,9 @@
     )
     for copy in copies:
         copy.start()
-    numbers_ref[...] = in_ref[pl.ds(64, 32, stride=65), :]
+    for row in range(32):
+        chunk = BACK_SLABS.index(row)
+        numbers_ref[row : row + 1, :] = in_ref[chunk * 65 + 64 : chunk * 65 + 65, :]
     same_ref[...] = jnp.zeros_like(same_ref)
     other_ref[...] = jnp.zeros_like(other_ref)
 
@@ -450,10 +484,17 @@
     return pltpu.with_memory_space_constraint(x, pltpu.HBM)
 
 
-def exchange(rows, axis, members):
+def exchange(rows, axis, members, order=None):
     count = rows.shape[0] // members
     chunks = (members, count, 128) if count % 8 == 0 else (members, 1, count * 128)
-    moved = lax.all_to_all(rows.reshape(chunks), axis, split_axis=0, concat_axis=0, tiled=True)
+    moved = lax.all_to_all(
+        rows.reshape(chunks),
+        axis,
+        split_axis=0,
+        concat_axis=0,
+        tiled=True,
+        axis_index_groups=None if order is None else [order],
+    )
     return moved.reshape(rows.shape)
 
 
@@ -474,8 +515,7 @@
     targets,
     counts,
 ):
-    forward, inverse = tables()
-    forward, inverse = jnp.asarray(forward), jnp.asarray(inverse)
+    modes, cells = list(range(MODES)), list(range(NG))
     shape = jax.ShapeDtypeStruct
     pre, cotan = pre.reshape(64, 64, 128), cotan.reshape(64, 64, 128)
 
@@ -495,20 +535,26 @@
     )(
         in_hbm(pre),
         in_hbm(cotan),
-        in_hbm(forward),
+        in_hbm(forward_table(OUT_SLABS, cells)),
         in_hbm(routes.reshape(1, 1024)),
         in_hbm(targets.reshape(1, 1024)),
     )
     code = code.reshape(1024)
 
-    columns = exchange(columns, "slab", 32)
-    rows = call(modes_x_kernel, shape((512, 128), F32), [VMEM, VMEM])(columns, forward)
+    columns = exchange(columns, "slab", 32, OUT_SLABS)
+    rows = call(modes_x_kernel, shape((512, 128), F32), [VMEM, VMEM])(columns, forward_table(modes, OUT_X))
     rows = exchange(rows, "grp", 8)
     rows = call(mix_kernel, shape((528, 128), F32), [VMEM] * 5)(
-        rows, spectral.reshape(8192, 128), forward, inverse, send_targets
+        rows,
+        spectral.reshape(8192, 128),
+        forward_table(modes, cells),
+        inverse_table(modes, cells),
+        send_targets,
     )
     rows = exchange(rows, "grp", 8)
-    columns = call(field_x_kernel, shape((2080, 128), F32), [VMEM, VMEM])(rows, inverse)
+    columns = call(field_x_kernel, shape((2080, 128), F32), [VMEM, VMEM])(
+        rows, inverse_table(modes, BACK_X)
+    )
 
     net_in = jnp.concatenate([kernel_inputs, jnp.ones((1, 1024), F32), jnp.zeros((1, 1024), F32)])
     first_layer = jnp.concatenate([w_in, b_in[None], jnp.zeros((1, 512), F32)])
@@ -554,7 +600,7 @@
         count,
     )
 
-    columns = exchange(columns, "slab", 32)
+    columns = exchange(columns, "slab", 32, BACK_SLABS)
     slots, numbers = call(
         slots_kernel,
         (shape((1024, 128), F32), shape((32, 128), F32)),
@@ -568,7 +614,7 @@
             pltpu.SMEM((4 * ROOM,), jnp.int32),
             pltpu.SemaphoreType.DMA((3,)),
         ],
-    )(columns, inverse, in_hbm(scale), in_hbm(shift), in_hbm(entries))
+    )(columns, inverse_table(BACK_SLABS, cells), in_hbm(scale), in_hbm(shift), in_hbm(entries))
     slots = exchange(slots, ("grp", "slab"), 256)
     return call(
         gather_kernel,

time: 139 us -> 137 us (0.986)
  blocking collectives: 94.3 us -> 90.2 us
  starting transfers between devices: 4.94 us -> 7.48 us
    all_to_all x4, blocking collectives: 94.3 us -> 90.2 us  [exchange(): lax.all_to_all(rows.reshape(chunks), axis, split_axis=0, concat_axis=0, t...]
    all_to_all x1, starting transfers between devices: 4.94 us -> 7.48 us  [exchange(): lax.all_to_all(rows.reshape(chunks), axis, split_axis=0, concat_axis=0, t...]
where the time goes in v3:
time: 137 us
  blocking collectives  90.2 us (66%)
  Pallas kernels  27.8 us (20%)
  waiting for transfers between devices  9.67 us (7%)
  starting transfers between devices  7.48 us (5%)
    all_to_all x4, blocking collectives, exchange(): lax.all_to_all(rows.reshape(chunks), axis, split_axis=0, concat_axis=0, t...  90.2 us
    pallas_call x1, Pallas kernels, local(): call(local_kernel, (pltpu.HBM((1024, 128), F32), pltpu.HBM((1024, 128), F...  10.3 us
    all_to_all x1, waiting for transfers between devices, exchange(): lax.all_to_all(rows.reshape(chunks), axis, split_axis=0, concat_axis=0, t...  9.67 us
    all_to_all x1, starting transfers between devices, exchange(): lax.all_to_all(rows.reshape(chunks), axis, split_axis=0, concat_axis=0, t...  7.48 us
    pallas_call x1, Pallas kernels, local(): call(kernel_net_kernel, shape((1024, 128), F32), [VMEM] * 6 + [SMEM, ANY])  4.53 us
    pallas_call x1, Pallas kernels, local(): call(modes_z_kernel, (shape((2048, 128), F32), shape((1, 1024), jnp.int32...  4.17 us
    pallas_call x1, Pallas kernels, local(): call(slots_kernel, (shape((1024, 128), F32), shape((32, 128), F32)), [VME...  3.25 us
  transfers between devices with their start and end apart: 1, of which 1 were waited for; matrix products, arithmetic and copies ran while one was open for 0% of the time, Pallas kernels for 11%

profile of v3, /device:TPU:1, one launch (start us, length us, event | category | flops | bytes accessed | tf_op | source)
XLA Modules:
  0.0 136.7 jit_solution(17511161583591413620)
XLA Ops:
  0.0 4.2 %shard_map.199 = (f32[2048,128]{1,0:T(8,128)S(1)}, s32[1,1024]{1,0:T(1,128)S(1)}, f32[8,256]{1,0:T(8,128)S(1)}) custom-call(bf16[64,64,128]{2,1,0:T(8,128)(2,1)} %bitcast.29, bf16[64,64,128]{2,1,0:T(8,128)(2,1)} %bitcast.31, bf16[128,256]{1,0:T(8,128)(2,1)} %constant.7.clone.table_hbm, s32[1,1024]{1,0:T(1,128)} %bitcast.49, s32[1,1024]{1,0:T(1,128)} %bitcast.50), custom_call_target="tpu_custom_call" | custom-call | tf_op jit(solution)/shard_map/pallas_call | solution.py:522
  4.2 0.0 copy-start.8
  4.2 37.1 %all_to_all.25 = f32[32,64,128]{2,1,0:T(8,128)S(1)} all-to-all(f32[32,64,128]{2,1,0:T(8,128)S(1)} %bitcast.38), channel_id=1, replica_groups={{15,14,13,12,11,10,9,8,7,6,5,4,3,2,1,0,31,30,29,28,27,26,25,24,23,22,21..., dimensions={0} | all-to-all | bytes 2097152 | tf_op jit(solution)/shard_map/all_to_all | solution.py:490
  41.3 0.6 shard_map.200
  41.9 12.7 %all_to_all.26 = f32[8,64,128]{2,1,0:T(8,128)S(1)} all-to-all(f32[8,64,128]{2,1,0:T(8,128)S(1)} %bitcast.39), channel_id=1, replica_groups=mesh['grp'=8,'slab'=32] {'grp'}, dimensions={0} | all-to-all | bytes 524288 | tf_op jit(solution)/shard_map/all_to_all | solution.py:490
  54.6 1.3 shard_map.201
  55.9 10.6 %all_to_all.27 = f32[8,1,8448]{2,1,0:T(1,128)S(1)} all-to-all(f32[8,1,8448]{2,1,0:T(1,128)S(1)} %bitcast.37), channel_id=1, replica_groups=mesh['grp'=8,'slab'=32] {'grp'}, dimensions={0} | all-to-all | bytes 540672 | tf_op jit(solution)/shard_map/all_to_all | solution.py:490
  66.5 1.6 %shard_map.202.after_hbm = f32[2080,128]{1,0:T(8,128)} custom-call(f32[528,128]{1,0:T(8,128)S(1)} %bitcast.36, bf16[128,192]{1,0:T(8,128)(2,1)S(1)} %copy-done.5), custom_call_target="tpu_custom_call" | custom-call | tf_op jit(solution)/shard_map/pallas_call | solution.py:555
  68.2 7.5 %all-to-all-start.3 = ((f32[32,1,8320]{2,1,0:T(1,128)}), f32[32,1,8320]{2,1,0:T(1,128)S(1)}, u32[]{:S(2)}, u32[]{:S(2)}) async-start(f32[32,1,8320]{2,1,0:T(1,128)} %bitcast.11), calls=%async_computation.3 | async-start | bytes 2129920 | tf_op jit(solution)/shard_map/all_to_all | solution.py:490
  75.7 0.1 pad.9.clone
  75.8 0.1 pad.8.clone
  75.9 0.1 maximum_bitcast_fusion.b_out_ref
  75.9 0.1 maximum_maximum_fusion.weight_ref
  76.1 0.1 maximum_maximum_fusion.2.w_in_ref
  76.1 0.1 maximum_maximum_fusion.1.in_ref
  76.2 0.2 shard_map.204
  76.4 0.3 copy-done.3
  76.7 4.5 %shard_map.203.kernel_ref = f32[1024,128]{1,0:T(8,128)S(1)} custom-call(f32[8,1024]{1,0:T(8,128)S(1)} %maximum_maximum_fusion.1.in_ref, f32[8,512]{1,0:T(8,128)S(1)} %maximum_maximum_fusion.2.w_in_ref, f32[512,256]{1,0:T(8,128)S(1)} %copy-done.3, f32[1,256]{1,0:T(1,128)S(1)} %bitcast.46, f32[128,256]{1,0:T(8,128)S(1)} %pad_maximum_fusion.w_out_ref, ...), custom_call_target="tpu_custom_call" | custom-call | tf_op jit(solution)/shard_map/pallas_call | solution.py:561
  81.3 10.3 %shard_map.205 = (f32[1024,128]{1,0:T(8,128)}, f32[1024,128]{1,0:T(8,128)}, s32[5120]{0:T(1024)S(1)}) custom-call(bf16[64,64,128]{2,1,0:T(8,128)(2,1)S(1)} %bitcast.30, bf16[64,64,128]{2,1,0:T(8,128)(2,1)S(1)} %bitcast.32, bf16[128,128]{1,0:T(8,128)(2,1)S(1)} %maximum_maximum_fusion.weight_ref, f32[1024,128]{1,0:T(8,128)S(1)} %shard_map.203.kernel_ref, ...), custom_call_target="tpu_custom_call" | custom-call | tf_op jit(solution)/shard_map/pallas_call | solution.py:585
  91.6 0.6 copy-done.9
  92.2 9.7 %all-to-all-done.3 = f32[32,1,8320]{2,1,0:T(1,128)S(1)} async-done(((f32[32,1,8320]{2,1,0:T(1,128)}), f32[32,1,8320]{2,1,0:T(1,128)S(1)}, u32[]{:S(2)}, u32[]{:S(2)}) %all-to-all-start.3) | async-done | bytes 1064992 | tf_op jit(solution)/shard_map/all_to_all | solution.py:490
  101.9 3.2 %shard_map.206 = (f32[1024,128]{1,0:T(8,128)S(1)}, f32[32,128]{1,0:T(8,128)S(1)}) custom-call(f32[2080,128]{1,0:T(8,128)S(1)} %bitcast.28, bf16[128,192]{1,0:T(8,128)(2,1)S(1)} %copy-done.4, f32[1024,128]{1,0:T(8,128)} %get-tuple-element.22.scale_hbm, f32[1024,128]{1,0:T(8,128)} %get-tuple-element.23.shift_hbm, s32[5120]{0:T(1024)} %copy-done.9), custom_call_target="tpu_custom_call" | custom-call | tf_op jit(solution)/shard_map/pallas_call | solution.py:604
  105.2 29.8 %all_to_all.28 = f32[256,1,512]{2,1,0:T(1,128)S(1)} all-to-all(f32[256,1,512]{2,1,0:T(1,128)S(1)} %bitcast.41), channel_id=1, replica_groups=mesh['grp'=8,'slab'=32] {'grp','slab'}, dimensions={0} | all-to-all | bytes 1048576 | tf_op jit(solution)/shard_map/all_to_all | solution.py:490
  134.9 1.8 %shard_map.207 = f32[64,1024]{1,0:T(8,128)} custom-call(f32[1024,128]{1,0:T(8,128)S(1)} %bitcast.35, f32[32,128]{1,0:T(8,128)S(1)} %get-tuple-element.26.numbers_ref), custom_call_target="tpu_custom_call" | custom-call | tf_op jit(solution)/shard_map/pallas_call | solution.py:619
  (36 shorter events, 0.1 us)
Async XLA Ops:
  4.2 37.1 %copy-start.8 = (bf16[128,256]{1,0:T(8,128)(2,1)S(1)}, bf16[128,256]{1,0:T(8,128)(2,1)}, u32[]{:S(2)}) copy-start(bf16[128,256]{1,0:T(8,128)(2,1)} %constant.18.clone.table_ref) | copy-start | bytes 196612
  4.2 50.4 %copy-start.2 = (bf16[1,4,32,64,128]{4,3,2,1,0:T(8,128)(2,1)S(1)}, bf16[1,4,32,64,128]{4,3,2,1,0:T(8,128)(2,1)}, u32[]{:S(2)}) copy-start(bf16[1,4,32,64,128]{4,3,2,1,0:T(8,128)(2,1)} %param.24) | copy-start | bytes 6291460
  41.3 13.3 %copy-start.6 = (bf16[128,256]{1,0:T(8,128)(2,1)S(1)}, bf16[128,256]{1,0:T(8,128)(2,1)}, u32[]{:S(2)}) copy-start(bf16[128,256]{1,0:T(8,128)(2,1)} %constant.19.clone.forward_ref) | copy-start | bytes 196612
  41.3 13.3 %copy-start.7 = (bf16[128,192]{1,0:T(8,128)(2,1)S(1)}, bf16[128,192]{1,0:T(8,128)(2,1)}, u32[]{:S(2)}) copy-start(bf16[128,192]{1,0:T(8,128)(2,1)} %constant.20.clone.inverse_ref) | copy-start | bytes 147460
  54.6 11.9 %copy-start.5 = (bf16[128,192]{1,0:T(8,128)(2,1)S(1)}, bf16[128,192]{1,0:T(8,128)(2,1)}, u32[]{:S(2)}) copy-start(bf16[128,192]{1,0:T(8,128)(2,1)} %constant.21.clone.table_ref) | copy-start | bytes 147460
  68.1 7.7 %copy-start.18 = (f32[64]{0:T(128)S(1)}, f32[64]{0:T(128)}, u32[]{:S(2)}) copy-start(f32[64]{0:T(128)} %param.30) | copy-start | bytes 772
  68.1 7.8 %copy-start.15 = (bf16[64,64]{1,0:T(8,128)(2,1)S(1)}, bf16[64,64]{1,0:T(8,128)(2,1)}, u32[]{:S(2)}) copy-start(bf16[64,64]{1,0:T(8,128)(2,1)} %param.23) | copy-start | bytes 24580
  68.1 7.9 %copy-start.13 = (f32[256,64]{0,1:T(8,128)S(1)}, f32[256,64]{0,1:T(8,128)}, u32[]{:S(2)}) copy-start(f32[256,64]{0,1:T(8,128)} %param.29) | copy-start | bytes 196612
  68.1 7.9 %copy-start.16 = (f32[6,512]{1,0:T(8,128)S(1)}, f32[6,512]{1,0:T(8,128)}, u32[]{:S(2)}) copy-start(f32[6,512]{1,0:T(8,128)} %param.25) | copy-start | bytes 36868
  68.1 7.9 %copy-start.17 = (f32[512]{0:T(512)S(1)}, f32[512]{0:T(512)}, u32[]{:S(2)}) copy-start(f32[512]{0:T(512)} %param.26) | copy-start | bytes 6148
  68.2 8.0 %copy-start.14 = (f32[6,1024]{1,0:T(8,128)S(1)}, f32[6,1024]{1,0:T(8,128)}, u32[]{:S(2)}) copy-start(f32[6,1024]{1,0:T(8,128)} %param.31) | copy-start | bytes 73732
  68.2 8.1 %copy-start.10 = (s32[1024]{0:T(1024)S(1)}, s32[1024]{0:T(1024)}, u32[]{:S(2)}) copy-start(s32[1024]{0:T(1024)} %voxel_ref.1) | copy-start | bytes 12292
  68.2 33.7 %all-to-all-start.3 = ((f32[32,1,8320]{2,1,0:T(1,128)}), f32[32,1,8320]{2,1,0:T(1,128)S(1)}, u32[]{:S(2)}, u32[]{:S(2)}) async-start(f32[32,1,8320]{2,1,0:T(1,128)} %bitcast.11), calls=%async_computation.3 | async-start | bytes 2129920 | tf_op jit(solution)/shard_map/all_to_all | solution.py:490
  75.7 1.0 copy-start.3
  75.7 1.0 copy-start.11
  75.7 1.0 copy-start.12
  76.7 4.5 %copy-start = (bf16[4,16,64,128]{3,2,1,0:T(8,128)(2,1)S(1)}, bf16[4,16,64,128]{3,2,1,0:T(8,128)(2,1)}, u32[]{:S(2)}) copy-start(bf16[4,16,64,128]{3,2,1,0:T(8,128)(2,1)} %param.21) | copy-start | bytes 3145732
  76.7 4.6 %copy-start.1 = (bf16[4,16,64,128]{3,2,1,0:T(8,128)(2,1)S(1)}, bf16[4,16,64,128]{3,2,1,0:T(8,128)(2,1)}, u32[]{:S(2)}) copy-start(bf16[4,16,64,128]{3,2,1,0:T(8,128)(2,1)} %param.22) | copy-start | bytes 3145732
  81.3 20.6 %copy-start.4 = (bf16[128,192]{1,0:T(8,128)(2,1)S(1)}, bf16[128,192]{1,0:T(8,128)(2,1)}, u32[]{:S(2)}) copy-start(bf16[128,192]{1,0:T(8,128)(2,1)} %constant.22.clone.table_ref) | copy-start | bytes 147460
  91.6 0.6 copy-start.9

commit v4 on v3

--- a/solution.py
+++ b/solution.py
@@ -14,7 +14,7 @@
 NG = 128
 MODES = 32
 CH = 64
-OUT_STEP, OUT_FIRST = 31, 15
+OUT_STEP, OUT_FIRST = 31, 23
 BACK_STEP, BACK_FIRST = 31, 15
 NN = (((1,), (0,)), ((), ()))
 NT = (((1,), (1,)), ((), ()))

time: 137 us -> 136 us (level)
  starting transfers between devices: 7.48 us -> 5.94 us
    all_to_all x1, starting transfers between devices: 7.48 us -> 5.94 us  [exchange(): lax.all_to_all(rows.reshape(chunks), axis, split_axis=0, concat_axis=0, t...]
where the time goes in v4:
time: 136 us
  blocking collectives  90.8 us (67%)
  Pallas kernels  27.8 us (20%)
  waiting for transfers between devices  9.67 us (7%)
  starting transfers between devices  5.94 us (4%)
    all_to_all x4, blocking collectives, exchange(): lax.all_to_all(rows.reshape(chunks), axis, split_axis=0, concat_axis=0, t...  90.8 us
    pallas_call x1, Pallas kernels, local(): call(local_kernel, (pltpu.HBM((1024, 128), F32), pltpu.HBM((1024, 128), F...  10.3 us
    all_to_all x1, waiting for transfers between devices, exchange(): lax.all_to_all(rows.reshape(chunks), axis, split_axis=0, concat_axis=0, t...  9.67 us
    all_to_all x1, starting transfers between devices, exchange(): lax.all_to_all(rows.reshape(chunks), axis, split_axis=0, concat_axis=0, t...  5.94 us
    pallas_call x1, Pallas kernels, local(): call(kernel_net_kernel, shape((1024, 128), F32), [VMEM] * 6 + [SMEM, ANY])  4.53 us
    pallas_call x1, Pallas kernels, local(): call(modes_z_kernel, (shape((2048, 128), F32), shape((1, 1024), jnp.int32...  4.17 us
    pallas_call x1, Pallas kernels, local(): call(slots_kernel, (shape((1024, 128), F32), shape((32, 128), F32)), [VME...  3.25 us
  transfers between devices with their start and end apart: 1, of which 1 were waited for; matrix products, arithmetic and copies ran while one was open for 0% of the time, Pallas kernels for 11%

profile of v4, /device:TPU:1, one launch (start us, length us, event | category | flops | bytes accessed | tf_op | source)
XLA Modules:
  0.0 135.8 jit_solution(9512167620140598299)
XLA Ops:
  0.0 4.2 %shard_map.199 = (f32[2048,128]{1,0:T(8,128)S(1)}, s32[1,1024]{1,0:T(1,128)S(1)}, f32[8,256]{1,0:T(8,128)S(1)}) custom-call(bf16[64,64,128]{2,1,0:T(8,128)(2,1)} %bitcast.29, bf16[64,64,128]{2,1,0:T(8,128)(2,1)} %bitcast.31, bf16[128,256]{1,0:T(8,128)(2,1)} %constant.7.clone.table_hbm, s32[1,1024]{1,0:T(1,128)} %bitcast.49, s32[1,1024]{1,0:T(1,128)} %bitcast.50), custom_call_target="tpu_custom_call" | custom-call | tf_op jit(solution)/shard_map/pallas_call | solution.py:522
  4.2 0.0 copy-start.8
  4.2 37.6 %all_to_all.25 = f32[32,64,128]{2,1,0:T(8,128)S(1)} all-to-all(f32[32,64,128]{2,1,0:T(8,128)S(1)} %bitcast.38), channel_id=1, replica_groups={{23,22,21,20,19,18,17,16,15,14,13,12,11,10,9,8,7,6,5,4,3,2,1,0,31,30,29..., dimensions={0} | all-to-all | bytes 2097152 | tf_op jit(solution)/shard_map/all_to_all | solution.py:490
  41.9 0.6 shard_map.200
  42.5 12.7 %all_to_all.26 = f32[8,64,128]{2,1,0:T(8,128)S(1)} all-to-all(f32[8,64,128]{2,1,0:T(8,128)S(1)} %bitcast.39), channel_id=1, replica_groups=mesh['grp'=8,'slab'=32] {'grp'}, dimensions={0} | all-to-all | bytes 524288 | tf_op jit(solution)/shard_map/all_to_all | solution.py:490
  55.2 1.3 shard_map.201
  56.5 10.6 %all_to_all.27 = f32[8,1,8448]{2,1,0:T(1,128)S(1)} all-to-all(f32[8,1,8448]{2,1,0:T(1,128)S(1)} %bitcast.37), channel_id=1, replica_groups=mesh['grp'=8,'slab'=32] {'grp'}, dimensions={0} | all-to-all | bytes 540672 | tf_op jit(solution)/shard_map/all_to_all | solution.py:490
  67.1 1.6 %shard_map.202.after_hbm = f32[2080,128]{1,0:T(8,128)} custom-call(f32[528,128]{1,0:T(8,128)S(1)} %bitcast.36, bf16[128,192]{1,0:T(8,128)(2,1)S(1)} %copy-done.5), custom_call_target="tpu_custom_call" | custom-call | tf_op jit(solution)/shard_map/pallas_call | solution.py:555
  68.8 5.9 %all-to-all-start.3 = ((f32[32,1,8320]{2,1,0:T(1,128)}), f32[32,1,8320]{2,1,0:T(1,128)S(1)}, u32[]{:S(2)}, u32[]{:S(2)}) async-start(f32[32,1,8320]{2,1,0:T(1,128)} %bitcast.11), calls=%async_computation.3 | async-start | bytes 2129920 | tf_op jit(solution)/shard_map/all_to_all | solution.py:490
  74.8 0.1 pad.9.clone
  74.8 0.1 pad.8.clone
  74.9 0.1 maximum_bitcast_fusion.b_out_ref
  75.0 0.1 maximum_maximum_fusion.weight_ref
  75.1 0.1 maximum_maximum_fusion.2.w_in_ref
  75.2 0.1 maximum_maximum_fusion.1.in_ref
  75.3 0.2 shard_map.204
  75.5 0.3 copy-done.3
  75.8 4.5 %shard_map.203.kernel_ref = f32[1024,128]{1,0:T(8,128)S(1)} custom-call(f32[8,1024]{1,0:T(8,128)S(1)} %maximum_maximum_fusion.1.in_ref, f32[8,512]{1,0:T(8,128)S(1)} %maximum_maximum_fusion.2.w_in_ref, f32[512,256]{1,0:T(8,128)S(1)} %copy-done.3, f32[1,256]{1,0:T(1,128)S(1)} %bitcast.46, f32[128,256]{1,0:T(8,128)S(1)} %pad_maximum_fusion.w_out_ref, ...), custom_call_target="tpu_custom_call" | custom-call | tf_op jit(solution)/shard_map/pallas_call | solution.py:561
  80.3 10.3 %shard_map.205 = (f32[1024,128]{1,0:T(8,128)}, f32[1024,128]{1,0:T(8,128)}, s32[5120]{0:T(1024)S(1)}) custom-call(bf16[64,64,128]{2,1,0:T(8,128)(2,1)S(1)} %bitcast.30, bf16[64,64,128]{2,1,0:T(8,128)(2,1)S(1)} %bitcast.32, bf16[128,128]{1,0:T(8,128)(2,1)S(1)} %maximum_maximum_fusion.weight_ref, f32[1024,128]{1,0:T(8,128)S(1)} %shard_map.203.kernel_ref, ...), custom_call_target="tpu_custom_call" | custom-call | tf_op jit(solution)/shard_map/pallas_call | solution.py:585
  90.7 0.6 copy-done.9
  91.3 9.7 %all-to-all-done.3 = f32[32,1,8320]{2,1,0:T(1,128)S(1)} async-done(((f32[32,1,8320]{2,1,0:T(1,128)}), f32[32,1,8320]{2,1,0:T(1,128)S(1)}, u32[]{:S(2)}, u32[]{:S(2)}) %all-to-all-start.3) | async-done | bytes 1064992 | tf_op jit(solution)/shard_map/all_to_all | solution.py:490
  101.0 3.2 %shard_map.206 = (f32[1024,128]{1,0:T(8,128)S(1)}, f32[32,128]{1,0:T(8,128)S(1)}) custom-call(f32[2080,128]{1,0:T(8,128)S(1)} %bitcast.28, bf16[128,192]{1,0:T(8,128)(2,1)S(1)} %copy-done.4, f32[1024,128]{1,0:T(8,128)} %get-tuple-element.22.scale_hbm, f32[1024,128]{1,0:T(8,128)} %get-tuple-element.23.shift_hbm, s32[5120]{0:T(1024)} %copy-done.9), custom_call_target="tpu_custom_call" | custom-call | tf_op jit(solution)/shard_map/pallas_call | solution.py:604
  104.2 29.8 %all_to_all.28 = f32[256,1,512]{2,1,0:T(1,128)S(1)} all-to-all(f32[256,1,512]{2,1,0:T(1,128)S(1)} %bitcast.41), channel_id=1, replica_groups=mesh['grp'=8,'slab'=32] {'grp','slab'}, dimensions={0} | all-to-all | bytes 1048576 | tf_op jit(solution)/shard_map/all_to_all | solution.py:490
  134.0 1.8 %shard_map.207 = f32[64,1024]{1,0:T(8,128)} custom-call(f32[1024,128]{1,0:T(8,128)S(1)} %bitcast.35, f32[32,128]{1,0:T(8,128)S(1)} %get-tuple-element.26.numbers_ref), custom_call_target="tpu_custom_call" | custom-call | tf_op jit(solution)/shard_map/pallas_call | solution.py:619
  (36 shorter events, 0.1 us)
Async XLA Ops:
  4.2 37.7 %copy-start.8 = (bf16[128,256]{1,0:T(8,128)(2,1)S(1)}, bf16[128,256]{1,0:T(8,128)(2,1)}, u32[]{:S(2)}) copy-start(bf16[128,256]{1,0:T(8,128)(2,1)} %constant.18.clone.table_ref) | copy-start | bytes 196612
  4.2 51.0 %copy-start.2 = (bf16[1,4,32,64,128]{4,3,2,1,0:T(8,128)(2,1)S(1)}, bf16[1,4,32,64,128]{4,3,2,1,0:T(8,128)(2,1)}, u32[]{:S(2)}) copy-start(bf16[1,4,32,64,128]{4,3,2,1,0:T(8,128)(2,1)} %param.24) | copy-start | bytes 6291460
  41.8 13.3 %copy-start.6 = (bf16[128,256]{1,0:T(8,128)(2,1)S(1)}, bf16[128,256]{1,0:T(8,128)(2,1)}, u32[]{:S(2)}) copy-start(bf16[128,256]{1,0:T(8,128)(2,1)} %constant.19.clone.forward_ref) | copy-start | bytes 196612
  41.8 13.3 %copy-start.7 = (bf16[128,192]{1,0:T(8,128)(2,1)S(1)}, bf16[128,192]{1,0:T(8,128)(2,1)}, u32[]{:S(2)}) copy-start(bf16[128,192]{1,0:T(8,128)(2,1)} %constant.20.clone.inverse_ref) | copy-start | bytes 147460
  55.2 11.9 %copy-start.5 = (bf16[128,192]{1,0:T(8,128)(2,1)S(1)}, bf16[128,192]{1,0:T(8,128)(2,1)}, u32[]{:S(2)}) copy-start(bf16[128,192]{1,0:T(8,128)(2,1)} %constant.21.clone.table_ref) | copy-start | bytes 147460
  68.7 6.2 %copy-start.18 = (f32[64]{0:T(128)S(1)}, f32[64]{0:T(128)}, u32[]{:S(2)}) copy-start(f32[64]{0:T(128)} %param.30) | copy-start | bytes 772
  68.7 6.3 %copy-start.15 = (bf16[64,64]{1,0:T(8,128)(2,1)S(1)}, bf16[64,64]{1,0:T(8,128)(2,1)}, u32[]{:S(2)}) copy-start(bf16[64,64]{1,0:T(8,128)(2,1)} %param.23) | copy-start | bytes 24580
  68.7 6.3 %copy-start.13 = (f32[256,64]{0,1:T(8,128)S(1)}, f32[256,64]{0,1:T(8,128)}, u32[]{:S(2)}) copy-start(f32[256,64]{0,1:T(8,128)} %param.29) | copy-start | bytes 196612
  68.7 6.4 %copy-start.16 = (f32[6,512]{1,0:T(8,128)S(1)}, f32[6,512]{1,0:T(8,128)}, u32[]{:S(2)}) copy-start(f32[6,512]{1,0:T(8,128)} %param.25) | copy-start | bytes 36868
  68.7 6.4 %copy-start.17 = (f32[512]{0:T(512)S(1)}, f32[512]{0:T(512)}, u32[]{:S(2)}) copy-start(f32[512]{0:T(512)} %param.26) | copy-start | bytes 6148
  68.7 6.5 %copy-start.14 = (f32[6,1024]{1,0:T(8,128)S(1)}, f32[6,1024]{1,0:T(8,128)}, u32[]{:S(2)}) copy-start(f32[6,1024]{1,0:T(8,128)} %param.31) | copy-start | bytes 73732
  68.8 6.5 %copy-start.10 = (s32[1024]{0:T(1024)S(1)}, s32[1024]{0:T(1024)}, u32[]{:S(2)}) copy-start(s32[1024]{0:T(1024)} %voxel_ref.1) | copy-start | bytes 12292
  68.8 32.2 %all-to-all-start.3 = ((f32[32,1,8320]{2,1,0:T(1,128)}), f32[32,1,8320]{2,1,0:T(1,128)S(1)}, u32[]{:S(2)}, u32[]{:S(2)}) async-start(f32[32,1,8320]{2,1,0:T(1,128)} %bitcast.11), calls=%async_computation.3 | async-start | bytes 2129920 | tf_op jit(solution)/shard_map/all_to_all | solution.py:490
  74.7 1.0 copy-start.3
  74.7 1.0 copy-start.11
  74.7 1.0 copy-start.12
  75.8 4.5 %copy-start = (bf16[4,16,64,128]{3,2,1,0:T(8,128)(2,1)S(1)}, bf16[4,16,64,128]{3,2,1,0:T(8,128)(2,1)}, u32[]{:S(2)}) copy-start(bf16[4,16,64,128]{3,2,1,0:T(8,128)(2,1)} %param.21) | copy-start | bytes 3145732
  75.8 4.6 %copy-start.1 = (bf16[4,16,64,128]{3,2,1,0:T(8,128)(2,1)S(1)}, bf16[4,16,64,128]{3,2,1,0:T(8,128)(2,1)}, u32[]{:S(2)}) copy-start(bf16[4,16,64,128]{3,2,1,0:T(8,128)(2,1)} %param.22) | copy-start | bytes 3145732
  80.3 20.6 %copy-start.4 = (bf16[128,192]{1,0:T(8,128)(2,1)S(1)}, bf16[128,192]{1,0:T(8,128)(2,1)}, u32[]{:S(2)}) copy-start(bf16[128,192]{1,0:T(8,128)(2,1)} %constant.22.clone.table_ref) | copy-start | bytes 147460
  90.7 0.6 copy-start.9
